TPU v7x, 32 devices: a whole 2x2x4 slice. The times are simulated.
32 devices in a mesh: dp: 8 (over z, y), tp: 4 (over x, core).
Axes of the slice: x: 2, y: 2, z: 4, core: 2. Of those that a mesh axis runs over, the one named last changes fastest.
Arguments:
- inputs: bfloat16 [32, 896, 512], P('dp', 'tp'), may hold values from -6 to 6
- dataset: int32 [32], P('dp'), may hold values from 0 to 3, as said below
- variate_mask: int32 [32, 896], P('dp'), may hold values from 0 to 1, as said below
- dataset_bias: bfloat16 [4, 512], replicated, may hold values from -3 to 3
- w_qkv: bfloat16 [3, 512, 512], P(None, None, 'tp'), may hold values from -0.25 to 0.25
- qv_bias: bfloat16 [2, 512], P(None, 'tp'), may hold values from -1.796875 to 1.796875
- w_out: bfloat16 [512, 512], P('tp'), may hold values from -1 to 1
- out_bias: bfloat16 [2, 512], replicated, may hold values from -1.796875 to 1.796875
- w_up: bfloat16 [512, 2048], P(None, 'tp'), may hold values from -0.25 to 0.25
- up_bias: bfloat16 [2048], P('tp'), may hold values from -1.796875 to 1.796875
- w_down: bfloat16 [2048, 512], P('tp'), may hold values from -0.125 to 0.125
- norm_gain: bfloat16 [2, 512], replicated, may hold values from 0.25 to 1.75
- norm_shift: bfloat16 [2, 512], replicated, may hold values from -1.796875 to 1.796875
- cotangent: bfloat16 [32, 896, 512], P('dp', 'tp'), may hold values from -6 to 6
Outputs:
- outputs: bfloat16 [32, 896, 512], P('dp', 'tp')
- input_grad: bfloat16 [32, 896, 512], P('dp', 'tp')
- dataset_bias_grad: float32 [4, 512], replicated
- w_qkv_grad: float32 [3, 512, 512], P(None, None, 'tp')
- qv_bias_grad: float32 [2, 512], P(None, 'tp')
- w_out_grad: float32 [512, 512], P('tp')
- out_bias_grad: float32 [2, 512], replicated
- w_up_grad: float32 [512, 2048], P(None, 'tp')
- up_bias_grad: float32 [2048], P('tp')
- w_down_grad: float32 [2048, 512], P('tp')
- norm_gain_grad: float32 [2, 512], replicated
- norm_shift_grad: float32 [2, 512], replicated
Inputs may be any that keep to these rules, and one draw needn't show every extreme that they name: In every aligned block of 4 windows (those of one index of dp) at least one window has dataset 3. `variate_mask`: variate 0 of every window is live. A window of dataset c has no live variate at or past entry c of (max(1, 7), max(1, 21), max(1, 321), max(1, 862)).
All inputs are finite; a program needn't handle non-finite values.
Results may differ from a plain program's by a relative error of at most 0.017.
Values may be sent and summed in bfloat16 or wider, within the bound.
A program may use at most 128 MiB of HBM per device.

v0:
```python
import math

import jax
import jax.numpy as jnp
from jax import lax
from jax.sharding import PartitionSpec as P

HD = 64


EPSILON = 1e-05
HIGHEST = lax.Precision.HIGHEST
NEG_FILL = -1e30


def layer_forward_norm(residual, gains, shifts):
    center = residual - jnp.mean(residual, axis=-1, keepdims=True)
    factor = lax.rsqrt(jnp.mean(center * center, axis=-1, keepdims=True) + EPSILON)
    normed = center * factor
    return (normed * gains + shifts, normed, factor)


def layer_back_norm(upstream, normed, factor, gains):
    scaled = upstream * gains
    result = factor * (
        scaled
        - jnp.mean(scaled, axis=-1, keepdims=True)
        - normed * jnp.mean(scaled * normed, axis=-1, keepdims=True)
    )
    return (result, jnp.sum(upstream * normed, axis=(0, 1)), jnp.sum(upstream, axis=(0, 1)))


def masked_scores(queries, key_rows, live_row):
    length = queries.shape[0]
    head_count = queries.shape[1] // HD
    q_heads = queries.reshape(length, head_count, HD)
    k_heads = key_rows.reshape(length, head_count, HD)
    scores = jnp.einsum("qhe,khe->hqk", q_heads, k_heads, preferred_element_type=jnp.float32) * (
        1.0 / math.sqrt(HD)
    )
    return (jnp.where(live_row[None, None, :] > 0.5, scores, NEG_FILL), q_heads, k_heads)


def attend_window(packed):
    queries, key_rows, value_rows, live_row = packed
    length = queries.shape[0]
    head_count = queries.shape[1] // HD
    scores, q_heads, k_heads = masked_scores(queries, key_rows, live_row)
    row_top = jnp.max(scores, axis=-1, keepdims=True)
    exponent = jnp.exp(scores - row_top)
    row_total = jnp.sum(exponent, axis=-1, keepdims=True)
    attn_prob = (exponent / row_total).astype(jnp.bfloat16)
    v_heads = value_rows.reshape(length, head_count, HD)
    mixture = jnp.einsum("hqk,khe->qhe", attn_prob, v_heads, preferred_element_type=jnp.float32)
    log_total = (row_top + jnp.log(row_total))[..., 0]
    return (mixture.reshape(length, head_count * HD).astype(jnp.bfloat16), log_total)


def attend_back(packed):
    queries, key_rows, value_rows, live_row, grad_out, log_total = packed
    length = queries.shape[0]
    head_count = queries.shape[1] // HD
    scores, q_heads, k_heads = masked_scores(queries, key_rows, live_row)
    attn_prob = jnp.exp(scores - log_total[..., None])
    prob_low = attn_prob.astype(jnp.bfloat16)
    v_heads = value_rows.reshape(length, head_count, HD)
    grad_heads = grad_out.reshape(length, head_count, HD)
    grad_values = jnp.einsum(
        "hqk,qhe->khe", prob_low, grad_heads, preferred_element_type=jnp.float32
    )
    grad_probs = jnp.einsum("qhe,khe->hqk", grad_heads, v_heads, preferred_element_type=jnp.float32)
    grad_scores = attn_prob * (grad_probs - jnp.sum(attn_prob * grad_probs, axis=-1, keepdims=True))
    score_low = grad_scores.astype(jnp.bfloat16)
    score_scale = 1.0 / math.sqrt(HD)
    grad_queries = (
        jnp.einsum("hqk,khe->qhe", score_low, k_heads, preferred_element_type=jnp.float32)
        * score_scale
    )
    grad_keys = (
        jnp.einsum("hqk,qhe->khe", score_low, q_heads, preferred_element_type=jnp.float32)
        * score_scale
    )
    joined = jnp.concatenate(
        [
            grad_queries.reshape(length, head_count * HD),
            grad_keys.reshape(length, head_count * HD),
            grad_values.reshape(length, head_count * HD),
        ],
        axis=-1,
    )
    return joined.astype(jnp.bfloat16)


def attention_forward(gathered, w_cat, b_cat, w_out, live_full):
    projected = (
        jnp.einsum("wvd,de->wve", gathered, w_cat, preferred_element_type=jnp.float32) + b_cat
    ).astype(jnp.bfloat16)
    col_width = w_out.shape[0]
    mixture, log_total = lax.map(
        attend_window,
        (
            projected[..., :col_width],
            projected[..., col_width : 2 * col_width],
            projected[..., 2 * col_width :],
            live_full,
        ),
    )
    part_sum = jnp.einsum("wvh,hd->wvd", mixture, w_out, preferred_element_type=jnp.float32)
    return (part_sum, projected, mixture, log_total)


def attention_back(grad_rows, gathered, projected, mixture, log_total, live_full, w_cat, w_out):
    w_out_g = jnp.einsum("wvh,wvd->hd", mixture, grad_rows, preferred_element_type=jnp.float32)
    grad_mixture = jnp.einsum(
        "wvd,hd->wvh", grad_rows, w_out, preferred_element_type=jnp.float32
    ).astype(jnp.bfloat16)
    col_width = w_out.shape[0]
    grad_proj = lax.map(
        attend_back,
        (
            projected[..., :col_width],
            projected[..., col_width : 2 * col_width],
            projected[..., 2 * col_width :],
            live_full,
            grad_mixture,
            log_total,
        ),
    )
    w_cat_g = jnp.einsum("wvd,wve->de", gathered, grad_proj, preferred_element_type=jnp.float32)
    b_cat_g = jnp.sum(grad_proj, axis=(0, 1), dtype=jnp.float32)
    part_sum = jnp.einsum("wve,de->wvd", grad_proj, w_cat, preferred_element_type=jnp.float32)
    return (part_sum, w_cat_g, b_cat_g, w_out_g)


def feed_forward(gathered, w_up, up_bias, w_down):
    pre_act = jnp.einsum(
        "wvd,df->wvf", gathered, w_up, preferred_element_type=jnp.float32
    ) + up_bias.astype(jnp.float32)
    act_full, gelu_back = jax.vjp(jax.nn.gelu, pre_act)
    act_low = act_full.astype(jnp.bfloat16)
    part_sum = jnp.einsum("wvf,fd->wvd", act_low, w_down, preferred_element_type=jnp.float32)
    return (part_sum, act_low, gelu_back)


def feed_back(grad_rows, gathered, act_low, gelu_back, w_up, w_down):
    w_down_g = jnp.einsum("wvf,wvd->fd", act_low, grad_rows, preferred_element_type=jnp.float32)
    grad_act = jnp.einsum("wvd,fd->wvf", grad_rows, w_down, preferred_element_type=jnp.float32)
    grad_pre = gelu_back(grad_act)[0]
    up_bias_g = jnp.sum(grad_pre, axis=(0, 1))
    grad_low = grad_pre.astype(jnp.bfloat16)
    w_up_g = jnp.einsum("wvd,wvf->df", gathered, grad_low, preferred_element_type=jnp.float32)
    part_sum = jnp.einsum("wvf,df->wvd", grad_low, w_up, preferred_element_type=jnp.float32)
    return (part_sum, w_up_g, up_bias_g, w_down_g)


def shards(
    inputs,
    dataset,
    variate_mask,
    dataset_bias,
    w_qkv,
    qv_bias,
    w_out,
    out_bias,
    w_up,
    up_bias,
    w_down,
    norm_gain,
    norm_shift,
    cotangent,
):
    my_rank = lax.axis_index("tp")
    one_hot = (
        dataset[:, None] == jnp.arange(dataset_bias.shape[0], dtype=jnp.int32)[None, :]
    ).astype(jnp.float32)
    offsets = jnp.dot(one_hot, dataset_bias.astype(jnp.float32), precision=HIGHEST)
    gains = norm_gain.astype(jnp.float32)
    shifts = norm_shift.astype(jnp.float32)
    biases = out_bias.astype(jnp.float32)
    rows_in, cot_in = (inputs, cotangent)
    qkv_used, qvb_used, out_used, up_used, upb_used, down_used = (
        w_qkv,
        qv_bias,
        w_out,
        w_up,
        up_bias,
        w_down,
    )
    row_start = my_rank * inputs.shape[1]
    row_span = rows_in.shape[1]
    win_live = variate_mask.astype(jnp.float32)
    live_rows = lax.dynamic_slice_in_dim(win_live, row_start, row_span, 1)
    col_width = out_used.shape[0]
    model_width = qkv_used.shape[1]
    w_cat = jnp.transpose(qkv_used, (1, 0, 2)).reshape(model_width, 3 * col_width)
    b_cat = jnp.concatenate(
        [
            qvb_used[0].astype(jnp.float32),
            jnp.zeros((col_width,), jnp.float32),
            qvb_used[1].astype(jnp.float32),
        ]
    )
    base_rows = rows_in.astype(jnp.float32) + offsets[:, None, :]
    act_in = base_rows.astype(jnp.bfloat16)
    act_full = lax.all_gather(act_in, "tp", axis=1, tiled=True)
    attn_part, projected, mixture, log_total = attention_forward(
        act_full, w_cat, b_cat, out_used, win_live
    )
    attn_sum = lax.psum_scatter(attn_part, "tp", scatter_dimension=1, tiled=True)
    hidden, normed_one, factor_one = layer_forward_norm(
        base_rows + attn_sum + biases[0], gains[0], shifts[0]
    )
    hidden_low = hidden.astype(jnp.bfloat16)
    hidden_full = lax.all_gather(hidden_low, "tp", axis=1, tiled=True)
    ffn_part, act_low, gelu_back = feed_forward(hidden_full, up_used, upb_used, down_used)
    ffn_sum = lax.psum_scatter(
        ffn_part.astype(jnp.bfloat16), "tp", scatter_dimension=1, tiled=True
    ).astype(jnp.float32)
    final_rows, normed_two, factor_two = layer_forward_norm(
        hidden + ffn_sum + biases[1], gains[1], shifts[1]
    )
    result_rows = (final_rows * live_rows[:, :, None]).astype(jnp.bfloat16)
    grad_final = cot_in.astype(jnp.float32) * live_rows[:, :, None]
    grad_two, gain_two, shift_two = layer_back_norm(grad_final, normed_two, factor_two, gains[1])
    grad_two_low = grad_two.astype(jnp.bfloat16)
    grad_two_full = lax.all_gather(grad_two_low, "tp", axis=1, tiled=True)
    ffn_back_part, up_grad, upb_grad, down_grad = feed_back(
        grad_two_full, hidden_full, act_low, gelu_back, up_used, down_used
    )
    ffn_back = lax.psum_scatter(
        ffn_back_part.astype(jnp.bfloat16), "tp", scatter_dimension=1, tiled=True
    ).astype(jnp.float32)
    grad_one, gain_one, shift_one = layer_back_norm(
        grad_two + ffn_back, normed_one, factor_one, gains[0]
    )
    grad_one_low = grad_one.astype(jnp.bfloat16)
    grad_one_full = lax.all_gather(grad_one_low, "tp", axis=1, tiled=True)
    attn_back_part, cat_grad, bcat_grad, out_grad = attention_back(
        grad_one_full, act_full, projected, mixture, log_total, win_live, w_cat, out_used
    )
    attn_back = lax.psum_scatter(
        attn_back_part.astype(jnp.bfloat16), "tp", scatter_dimension=1, tiled=True
    ).astype(jnp.float32)
    grad_base = grad_one + attn_back
    input_low = grad_base.astype(jnp.bfloat16)
    bias_grad = jnp.dot(one_hot.T, jnp.sum(grad_base, axis=1), precision=HIGHEST)
    qkv_grad = jnp.transpose(cat_grad.reshape(model_width, 3, col_width), (1, 0, 2))
    qvb_grad = jnp.stack([bcat_grad[:col_width], bcat_grad[2 * col_width :]])
    weight_totals = lax.psum((qkv_grad, qvb_grad, out_grad, up_grad, upb_grad, down_grad), "dp")
    shared = lax.psum(
        (
            bias_grad,
            jnp.stack([gain_one, gain_two]),
            jnp.stack([shift_one, shift_two]),
            jnp.stack([jnp.sum(grad_one, axis=(0, 1)), jnp.sum(grad_two, axis=(0, 1))]),
        ),
        ("dp", "tp"),
    )
    return (
        result_rows,
        input_low,
        shared[0],
        weight_totals[0],
        weight_totals[1],
        weight_totals[2],
        shared[3],
        weight_totals[3],
        weight_totals[4],
        weight_totals[5],
        shared[1],
        shared[2],
    )


def solution(mesh):
    in_specs = (
        P("dp", "tp", None),
        P("dp"),
        P("dp", None),
        P(),
        P(None, None, "tp"),
        P(None, "tp"),
        P("tp", None),
        P(),
        P(None, "tp"),
        P("tp"),
        P("tp", None),
        P(),
        P(),
        P("dp", "tp", None),
    )
    out_specs = (
        P("dp", "tp", None),
        P("dp", "tp", None),
        P(),
        P(None, None, "tp"),
        P(None, "tp"),
        P("tp", None),
        P(),
        P(None, "tp"),
        P("tp"),
        P("tp", None),
        P(),
        P(),
    )
    return jax.shard_map(shards, mesh=mesh, in_specs=in_specs, out_specs=out_specs, check_vma=False)
```

profile of v0, /device:TPU:0, one launch (start us, length us, event | category | flops | bytes accessed | tf_op | source)
XLA Modules:
  0.0 613.0 jit_solution(5548335376186596348)
XLA Ops:
  13.2 31.6 %all-gather.5.cloned.1.call-done = bf16[4,896,512]{2,1,0:T(8,128)(2,1)} async-done(((bf16[4,224,512]{2,1,0:T(8,128)(2,1)}), bf16[4,896,512]{2,1,0:T(8,128)(2,1)}) %all-gather.5.cloned.1.call-update) | async-done | bytes 3670032 | tf_op jit(solution)/shard_map/all_gather | solution.py:205
  44.8 4.1 add_convert_fusion
  53.3 23.3 %while.22 = (s32[]{:T(128)}, bf16[4,896,128]{1,2,0:T(8,128)(2,1)}, f32[4,2,896]{2,1,0:T(2,128)S(1)}, bf16[4,896,128]{1,2,0:T(8,128)(2,1)S(1)}, f32[4,896]{1,0:T(...) while((s32[]{:T(128)}, bf16[4,896,128]{1,2,0:T(8,128)(2,1)}, ...), condition=%wide.region_3.4_spmd, body=%wide.region_0.3_spmd.sunk | while | flops 430423168 | bytes 22084720 | solution.py:99
  76.6 5.9 fusion.42
  83.3 64.9 %reduce-scatter.5.cloned.1.call-done = f32[4,224,512]{2,1,0:T(8,128)} async-done(((f32[4,896,512]{2,1,0:T(8,128)}), f32[4,224,512]{2,1,0:T(8,128)}) %reduce-scatter.5.cloned.1.call-update) | async-done | bytes 1835024 | tf_op jit(solution)/shard_map/reduce_scatter | solution.py:209
  152.3 31.4 %all-gather.7.cloned.1.call-done = bf16[4,896,512]{2,1,0:T(8,128)(2,1)} async-done(((bf16[4,224,512]{2,1,0:T(8,128)(2,1)}), bf16[4,896,512]{2,1,0:T(8,128)(2,1)}) %all-gather.7.cloned.1.call-update) | async-done | bytes 3670032 | tf_op jit(solution)/shard_map/all_gather | solution.py:214
  183.8 4.2 fusion.39
  191.0 4.4 convolution_convert_fusion.2
  195.5 41.3 %reduce-scatter.7.cloned.1.call-done = bf16[4,224,512]{2,1,0:T(8,128)(2,1)} async-done(((bf16[4,896,512]{2,1,0:T(8,128)(2,1)}), bf16[4,224,512]{2,1,0:T(8,128)(2,1)}) %reduce-scatter.7.cloned.1.call-update) | async-done | bytes 917520 | tf_op jit(solution)/shard_map/reduce_scatter | solution.py:216
  242.8 31.6 %all-gather.9.cloned.1.call-done = bf16[4,896,512]{2,1,0:T(8,128)(2,1)} async-done(((bf16[4,224,512]{2,1,0:T(8,128)(2,1)}), bf16[4,896,512]{2,1,0:T(8,128)(2,1)}) %all-gather.9.cloned.1.call-update) | async-done | bytes 3670032 | tf_op jit(solution)/shard_map/all_gather | solution.py:226
  274.4 9.3 %fusion.58 = (f32[512]{0:T(512)S(1)}, bf16[4,896,512]{2,1,0:T(8,128)(2,1)S(1)}) fusion(f32[4,896,512]{2,1,0:T(8,128)} %copy-done.5, f32[512]{0:T(512)S(1)} %convert_element_type.131, bf16[4,896,512]{2,1,0:T(8,128)(2,1)} %all-gather.9.cloned.1.call-done, bf16[512,512]{1,0:T(8,128)(2,1)S(1)} %copy-done), kind=kOutput, calls=%fused_computation.123 | convolution fusion | flops 1919417856 | bytes 15208448 | tf_op jit(solution)/shard_map/wvd,fd->wvf/dot_general | solution.py:147
  285.5 4.1 convolution_convert_fusion.1
  289.9 41.1 %reduce-scatter.9.cloned.1.call-done = bf16[4,224,512]{2,1,0:T(8,128)(2,1)} async-done(((bf16[4,896,512]{2,1,0:T(8,128)(2,1)}), bf16[4,224,512]{2,1,0:T(8,128)(2,1)}) %reduce-scatter.9.cloned.1.call-update) | async-done | bytes 917520 | tf_op jit(solution)/shard_map/reduce_scatter | solution.py:230
  331.0 3.0 multiply_reduce_fusion.2
  336.0 31.6 %all-gather.11.cloned.1.call-done = bf16[4,896,512]{2,1,0:T(8,128)(2,1)} async-done(((bf16[4,224,512]{2,1,0:T(8,128)(2,1)}), bf16[4,896,512]{2,1,0:T(8,128)(2,1)}) %all-gather.11.cloned.1.call-update) | async-done | bytes 3670032 | tf_op jit(solution)/shard_map/all_gather | solution.py:237
  367.7 3.1 convolution_convert_fusion.3
  370.8 44.7 %while.23 = (s32[]{:T(128)}, bf16[4,896,384]{1,2,0:T(8,128)(2,1)}, bf16[4,896,128]{1,2,0:T(8,128)(2,1)S(1)}, f32[4,896]{1,0:T(4,128)S(1)}, bf16[4,896,128]{1,2,0...) while((s32[]{:T(128)}, bf16[4,896,384]{1,2,0:T(8,128)(2,1)}, ...), condition=%wide.region_17.18_spmd, body=%wide.region_15.17_spmd.sunk | while | flops 1054325888 | bytes 54190204 | solution.py:118
  415.5 5.7 convolution_convert_fusion
  421.5 6.3 %fusion.31 = f32[512,512]{1,0:T(8,128)} fusion(bf16[4,896,512]{2,1,0:T(8,128)(2,1)} %all-gather.7.cloned.1.call-done, bf16[4,896,512]{2,1,0:T(8,128)(2,1)} %copy-done.9), kind=kOutput, calls=%fused_computation.78 | convolution fusion | flops 1879048192 | bytes 8388608 | tf_op jit(solution)/shard_map/wvd,wvf->df/dot_general | solution.py:151
  427.9 8.5 %convolution_bitcast_fusion = f32[512,512]{1,0:T(8,128)} fusion(bf16[4,896,512]{2,1,0:T(8,128)(2,1)S(1)} %copy-done.22, f32[4,896,512]{2,1,0:T(8,128)} %copy-done.5, f32[512]{0:T(512)S(1)} %convert_element_type.131), kind=kOutput, calls=%fused_computation.77 | convolution fusion | flops 1897398272 | bytes 12060672 | tf_op jit(solution)/shard_map/wvf,wvd->fd/dot_general | solution.py:146
  439.1 3.8 convolution_bitcast_fusion.1
  445.3 22.0 %all-reduce.1 = (f32[2,128]{1,0:T(2,128)}, f32[512]{0:T(512)}) all-reduce(f32[2,128]{1,0:T(2,128)S(1)} %pad_maximum_fusion.4, f32[512]{0:T(512)S(1)} %get-tuple-element.207), channel_id=1, replica_groups=mesh['dp'=8,'tp'=4] {'dp'}, use_global_device_ids=true, to_apply=%region_23.24 | all-reduce | flops 768 | bytes 6144 | tf_op jit(solution)/shard_map/psum | solution.py:249
  470.1 41.4 %all-reduce = (f32[4,512]{1,0:T(4,128)}, f32[2,512]{1,0:T(2,128)}, f32[2,512]{1,0:T(2,128)}, f32[2,512]{1,0:T(2,128)}) all-reduce(f32[4,512]{1,0:T(4,128)S(1)} %fusion.44, f32[2,512]{1,0:T(2,128)S(1)} %pad_maximum_fusion, f32[2,512]{1,0:T(2,128)S(1)} %pad_maximum_fusion.1, ...), channel_id=1, replica_groups=mesh['dp'=8,'tp'=4] {'dp','tp'}, use_global_device_ids=true, to_apply=%region_20.21 | all-reduce | flops 5120 | bytes 40960 | tf_op jit(solution)/shard_map/psum | solution.py:250
  511.5 87.5 %all-reduce.5.cloned.1.call-done = (f32[3,512,128]{2,1,0:T(8,128)}, f32[128,512]{1,0:T(8,128)}, f32[512,512]{1,0:T(8,128)}, f32[512,512]{1,0:T(8,128)}) async-done(((f32[3,512,128]{2,1,0:T(8,128)}, f32[128,512]{1,0:T(8,128)}, f32[512,512]{1,0:T(8,128)}, f32[512,512]{1,0:T(8,128)}), (f32[3,512,128]{2,1,0:T(8,128)}, f32[128,512]{1,0:T(8,128)}, f32[512,512]{1,0:T(8,128)}, ...) | async-done | bytes 3145744 | tf_op jit(solution)/shard_map/psum | solution.py:249
  (199 shorter events, 111.0 us)
Async XLA Ops:
  7.2 183.8 %copy-start = (bf16[512,512]{1,0:T(8,128)(2,1)S(1)}, bf16[512,512]{1,0:T(8,128)(2,1)}, u32[]{:S(2)}) copy-start(bf16[512,512]{1,0:T(8,128)(2,1)} %param.28) | copy-start | bytes 1572868
  7.2 37.6 %all-gather.5.cloned.1.call-start = ((), (), s32[]{:S(2)}) async-start(), calls=%async_computation.4 | async-start | bytes 4587520 | tf_op jit(solution)/shard_map/all_gather | solution.py:205
  10.5 137.7 %reduce-scatter.5.cloned.1.call-start = ((), (), s32[]{:S(2)}) async-start(), calls=%async_computation.5 | async-start | bytes 9175040 | tf_op jit(solution)/shard_map/reduce_scatter | solution.py:209
  12.4 36.5 %copy-start.15 = (bf16[3,512,128]{1,2,0:T(8,128)(2,1)}, bf16[3,512,128]{1,2,0:T(8,128)(2,1)S(1)}, u32[]{:S(2)}) copy-start(bf16[3,512,128]{1,2,0:T(8,128)(2,1)S(1)} %copy.45) | copy-start | bytes 1179652
  53.3 23.3 %copy-start.13 = (bf16[128,512]{1,0:T(8,128)(2,1)S(1)}, bf16[128,512]{1,0:T(8,128)(2,1)}, u32[]{:S(2)}) copy-start(bf16[128,512]{1,0:T(8,128)(2,1)} %param.24) | copy-start | bytes 393220
  76.6 6.0 copy-start.3
  76.6 6.0 copy-start.4
  82.6 101.2 %all-gather.7.cloned.1.call-start = ((), (), s32[]{:S(2)}) async-start(), calls=%async_computation.6 | async-start | bytes 4587520 | tf_op jit(solution)/shard_map/all_gather | solution.py:214
  152.1 84.7 %reduce-scatter.7.cloned.1.call-start = ((), (), s32[]{:S(2)}) async-start(), calls=%async_computation.7 | async-start | bytes 4587520 | tf_op jit(solution)/shard_map/reduce_scatter | solution.py:216
  195.4 79.0 %all-gather.9.cloned.1.call-start = ((), (), s32[]{:S(2)}) async-start(), calls=%async_computation.8 | async-start | bytes 4587520 | tf_op jit(solution)/shard_map/all_gather | solution.py:226
  242.7 88.3 %reduce-scatter.9.cloned.1.call-start = ((), (), s32[]{:S(2)}) async-start(), calls=%async_computation.9 | async-start | bytes 4587520 | tf_op jit(solution)/shard_map/reduce_scatter | solution.py:230
  274.4 11.1 %copy-start.14 = (bf16[512,512]{1,0:T(8,128)(2,1)S(1)}, bf16[512,512]{1,0:T(8,128)(2,1)}, u32[]{:S(2)}) copy-start(bf16[512,512]{1,0:T(8,128)(2,1)} %param.26) | copy-start | bytes 1572868
  289.6 78.0 %all-gather.11.cloned.1.call-start = ((), (), s32[]{:S(2)}) async-start(), calls=%async_computation.10 | async-start | bytes 4587520 | tf_op jit(solution)/shard_map/all_gather | solution.py:237
  331.0 3.0 copy-start.10
  336.0 131.4 %reduce-scatter.11.cloned.1.call-start = ((), (), s32[]{:S(2)}) async-start(), calls=%async_computation.11 | async-start | bytes 4587520 | tf_op jit(solution)/shard_map/reduce_scatter | solution.py:241
  370.8 44.7 %copy-start.16 = (bf16[3,512,128]{1,2,0:T(8,128)(2,1)S(1)}, bf16[3,512,128]{1,2,0:T(8,128)(2,1)}, u32[]{:S(2)}) copy-start(bf16[3,512,128]{1,2,0:T(8,128)(2,1)} %copy-done.15) | copy-start | bytes 1179652
  421.2 177.8 %all-reduce.5.cloned.1.call-start = ((), (), s32[]{:S(2)}) async-start(), calls=%async_computation.12 | async-start | bytes 6291456 | tf_op jit(solution)/shard_map/psum | solution.py:249
  421.5 6.4 %copy-start.22 = (bf16[4,896,512]{2,1,0:T(8,128)(2,1)S(1)}, bf16[4,896,512]{2,1,0:T(8,128)(2,1)}, u32[]{:S(2)}) copy-start(bf16[4,896,512]{2,1,0:T(8,128)(2,1)} %all-gather.9.cloned.1.call-done) | copy-start | bytes 11010052
  427.9 8.5 %copy-start.11 = (bf16[4,896,384]{1,2,0:T(8,128)(2,1)S(1)}, bf16[4,896,384]{1,2,0:T(8,128)(2,1)}, u32[]{:S(2)}) copy-start(bf16[4,896,384]{1,2,0:T(8,128)(2,1)} %get-tuple-element.94) | copy-start | bytes 8257540
  427.9 8.5 %copy-start.21 = (bf16[4,896,512]{2,1,0:T(8,128)(2,1)S(1)}, bf16[4,896,512]{2,1,0:T(8,128)(2,1)}, u32[]{:S(2)}) copy-start(bf16[4,896,512]{2,1,0:T(8,128)(2,1)} %all-gather.5.cloned.1.call-done) | copy-start | bytes 11010052
  442.9 24.5 %copy-start.6 = (f32[4,224,512]{2,1,0:T(8,128)S(1)}, f32[4,224,512]{2,1,0:T(8,128)}, u32[]{:S(2)}) copy-start(f32[4,224,512]{2,1,0:T(8,128)} %get-tuple-element.177) | copy-start | bytes 5505028
  442.9 26.9 %copy-start.23 = (s32[4]{0:T(128)S(1)}, s32[4]{0:T(128)}, u32[]{:S(2)}) copy-start(s32[4]{0:T(128)} %param.19) | copy-start | bytes 52
  467.3 138.7 %copy-start.1 = (bf16[512,512]{1,0:T(8,128)(2,1)S(1)}, bf16[512,512]{1,0:T(8,128)(2,1)}, u32[]{:S(2)}) copy-start(bf16[512,512]{1,0:T(8,128)(2,1)} %param.28) | copy-start | bytes 1572868
  599.0 6.1 copy-start.12
  (9 other events, 17.0 us)
Sparse Core Ops, SparseCore 0:
  10.6 34.1 all-gather.4
  82.7 65.4 reduce-scatter.4
  152.2 31.5 all-gather.6
  195.5 41.2 reduce-scatter.6
  242.8 31.4 all-gather.8
  289.8 41.2 reduce-scatter.8
  336.1 31.5 all-gather.10
  421.4 41.2 reduce-scatter.10
  467.6 131.3 all-reduce.4
where the time goes:
time: 621 us; the launch traced here: 613 us
  waiting for transfers between devices  361 us (58%)
  matrix products  101 us (16%)
  blocking collectives  63.4 us (10%)
  other arithmetic  43.1 us (7%)
  local copies, waits for them, and re-layouts  27.7 us (4%)
  between operations  14.6 us (2%)
    psum x1, waiting for transfers between devices, shards(): lax.psum((qkv_grad, qvb_grad, out_grad, up_grad, upb_grad, down_grad), 'dp')  87.5 us
    reduce_scatter x1, waiting for transfers between devices, shards(): lax.psum_scatter(attn_part, 'tp', scatter_dimension=1, tiled=True)  64.9 us
    psum x1, blocking collectives, shards(): lax.psum((bias_grad, jnp.stack([gain_one, gain_two]), jnp.stack([shift_on...  41.4 us
    reduce_scatter x1, waiting for transfers between devices, shards(): lax.psum_scatter(ffn_part.astype(jnp.bfloat16), 'tp', scatter_dimension=1...  41.3 us
    reduce_scatter x1, waiting for transfers between devices, shards(): lax.psum_scatter(ffn_back_part.astype(jnp.bfloat16), 'tp', scatter_dimens...  41.1 us
    all_gather x1, waiting for transfers between devices, shards(): act_full = lax.all_gather(act_in, 'tp', axis=1, tiled=True)  31.6 us
    all_gather x1, waiting for transfers between devices, shards(): grad_one_full = lax.all_gather(grad_one_low, 'tp', axis=1, tiled=True)  31.6 us
    all_gather x1, waiting for transfers between devices, shards(): grad_two_full = lax.all_gather(grad_two_low, 'tp', axis=1, tiled=True)  31.6 us
  transfers between devices with their start and end apart: 9, of which 8 were waited for; matrix products, arithmetic and copies ran while one was open for 5% of the time, Pallas kernels for 0%

commit v1 on v0

v1 whole, which is shorter than its diff:
```python
import functools
import math

import jax
import jax.numpy as jnp
from jax import lax
from jax.experimental import pallas as pl
from jax.experimental.pallas import tpu as pltpu
from jax.sharding import PartitionSpec as P

HD = 64
EPSILON = 1e-05
NEG_FILL = -1e30
BF = jnp.bfloat16
F32 = jnp.float32
MESH = pl.DeviceIdType.MESH
GELU_C = math.sqrt(2.0 / math.pi)
LANES = 128


def nn(a, b):
    return jnp.dot(a, b, preferred_element_type=F32)


def nt(a, b):
    return lax.dot_general(a, b, (((1,), (1,)), ((), ())), preferred_element_type=F32)


def tn(a, b):
    return lax.dot_general(a, b, (((0,), (0,)), ((), ())), preferred_element_type=F32)


def flip(value, k):
    low = lax.rem(lax.rem(value, 2) + k % 2, 2) if isinstance(k, int) else lax.rem(lax.rem(value, 2) + lax.rem(k, 2), 2)
    high = lax.rem(lax.div(value, 2) + (k // 2 if isinstance(k, int) else lax.div(k, 2)), 2)
    return high * 2 + low


def aligned(index, size):
    return pl.ds(pl.multiple_of(index * size, size), size)


def kernel(
    quad, rest_n,
    x_in, cot_in, dataset, mask, dbias, w_qkv, qvb, w_out, obias, w_up, upb, w_down, gain, shift,
    out_rows, ig_rows, g_qkv, g_out, g_up, g_down, g_dbias, g_gain, g_shift, g_obias, g_upb, g_qvb,
    X, COT, WP, WO, WU, WD, SB, ACT, QA, KA, VA, PR, MIX, LINV, N1, HL, ACT2, GP, ACC, G2L, LIVE,
    G, RC, RX, RQ, RE, SM, SMT, SMQ, SMR,
    s_own, s_x, r_x, s_c, r_c, s_w, r_w, s_b, r_b, s_out, r_out, s_ig, r_ig, s_loc,
    s_rc, r_rc, s_rx, r_rx, s_rq, r_rq, s_re, r_re, s_ag, r_ag, s_sm, r_sm, s_res,
):
    dp = lax.axis_index("dp")
    tp = lax.axis_index("tp")
    q_id = lax.rem(dp, quad)
    r_id = lax.div(dp, quad)
    rows = x_in.shape[1]
    total, width = X.shape
    half = total // 2
    x_id = lax.div(tp, 2)

    def tp_peer(k):
        return (dp, flip(tp, k))

    def quad_at(j):
        return lax.rem(q_id + j + quad, quad)

    def quad_peer(j):
        return (r_id * quad + quad_at(j), tp)

    def rest_peer(j):
        return (lax.rem(r_id + j, rest_n) * quad + q_id, tp)

    def rcopy(src, dst, ss, rs, dev):
        return pltpu.make_async_remote_copy(
            src_ref=src, dst_ref=dst, send_sem=ss, recv_sem=rs, device_id=dev, device_id_type=MESH
        )

    barrier = pltpu.get_barrier_semaphore()
    peers = [tp_peer(k) for k in (1, 2, 3)] + [quad_peer(j) for j in range(1, quad)]
    peers += [rest_peer(j) for j in range(1, rest_n)]
    for peer in peers:
        pl.semaphore_signal(barrier, inc=1, device_id=peer, device_id_type=MESH)

    own = [pltpu.make_async_copy(x_in.at[tp], X.at[aligned(tp, rows), :], s_own.at[0])]
    for i in range(3):
        own.append(pltpu.make_async_copy(w_qkv.at[i], WP.at[tp, :, pl.ds(i * LANES, LANES)], s_own.at[1 + i]))
    own.append(pltpu.make_async_copy(w_out, WO.at[aligned(tp, LANES), :], s_own.at[4]))
    own.append(pltpu.make_async_copy(w_up, WU.at[tp], s_own.at[5]))
    own.append(pltpu.make_async_copy(w_down, WD.at[tp], s_own.at[6]))
    own.append(pltpu.make_async_copy(cot_in.at[tp], COT.at[aligned(tp, rows), :], s_own.at[7]))
    for copy in own:
        copy.start()

    SB[tp, 0:2, :] = qvb[...].astype(F32)
    SB[tp, 2:6, :] = upb[...].astype(F32)
    pl.semaphore_wait(barrier, len(peers))

    def weight_slices(t):
        return [WP.at[t, :, pl.ds(i * LANES, LANES)] for i in range(3)] + [
            WO.at[aligned(t, LANES), :], WU.at[t], WD.at[t]
        ]

    w_src = [w_qkv.at[0], w_qkv.at[1], w_qkv.at[2], w_out, w_up, w_down]
    w_dst = weight_slices(tp)

    def w_send(i, k):
        return rcopy(w_src[i], w_dst[i], s_w.at[i, k], r_w.at[i, k], tp_peer(k))

    def w_wait(i, k):
        dst = weight_slices(flip(tp, k))[i]
        rcopy(dst, dst, s_w.at[i, k], r_w.at[i, k], tp_peer(k)).wait_recv()

    def w_forward(i):
        dst = weight_slices(flip(tp, 2))[i]
        return rcopy(dst, dst, s_w.at[i, 3], r_w.at[i, 3], tp_peer(1))

    def rows_copy(src, dst, ss, rs, k):
        return rcopy(src.at[flip(tp, k)], dst.at[aligned(tp, rows), :], ss.at[k], rs.at[k], tp_peer(k))

    def rows_wait(dst, ss, rs, k):
        there = dst.at[aligned(flip(tp, k), rows), :]
        rcopy(there, there, ss.at[k], rs.at[k], tp_peer(k)).wait_recv()

    def sb_copy(k):
        return rcopy(SB.at[tp], SB.at[tp], s_b.at[k], r_b.at[k], tp_peer(k))

    sends = []
    for k in (1, 2, 3):
        sends.append(sb_copy(k))
    for i in range(3):
        sends.append(w_send(i, 2))
        sends.append(w_send(i, 1))
    for k in (2, 3, 1):
        sends.append(rows_copy(x_in, X, s_x, r_x, k))
    for i in (3, 4, 5):
        sends.append(w_send(i, 2))
        sends.append(w_send(i, 1))
    for k in (2, 3, 1):
        sends.append(rows_copy(cot_in, COT, s_c, r_c, k))
    for copy in sends:
        copy.start()

    live_row = mask[pl.ds(tp, 1), :].astype(F32)
    LIVE[:, 0:8] = jnp.transpose(jnp.broadcast_to(live_row, (8, total)))
    ds_here = dataset[tp]
    off = jnp.zeros((1, X.shape[1]), F32)
    for c in range(dbias.shape[0]):
        off = off + jnp.where(ds_here == c, 1.0, 0.0) * dbias[c : c + 1, :].astype(F32)

    for copy in own:
        copy.wait()
    for k in (1, 2, 3):
        there = SB.at[flip(tp, k)]
        rcopy(there, there, s_b.at[k], r_b.at[k], tp_peer(k)).wait_recv()

    lane = lax.broadcasted_iota(jnp.int32, (half, LANES), 1)
    upper = lane >= HD
    one = jnp.ones((), BF)
    zero = jnp.zeros((), BF)

    def project(hh, first):
        rr = aligned(hh, half)
        ACT[rr, :] = (X[rr, :].astype(F32) + off).astype(BF)
        fill = jnp.where(LIVE[rr, 0:1] > 0.5, 0.0, NEG_FILL).astype(BF)
        fill = jnp.broadcast_to(fill, (half, LANES))

        def shard(k, carry):
            t = flip(tp, k)
            if first:
                @pl.when(k == 1)
                def _():
                    for i in range(3):
                        w_wait(i, 1)

                @pl.when(k == 2)
                def _():
                    for i in range(3):
                        w_wait(i, 2)
                        w_forward(i).start()

                @pl.when(k == 3)
                def _():
                    for i in range(3):
                        w_wait(i, 3)

            qkv = nn(ACT[rr, :], WP[t])
            query = (qkv[:, :LANES] + SB[t, 0:1, :]).astype(BF) * BF(0.125)
            keys = qkv[:, LANES : 2 * LANES].astype(BF)
            vals = (qkv[:, 2 * LANES :] + SB[t, 1:2, :]).astype(BF)
            QA[2 * t, rr, :] = jnp.where(upper, jnp.where(lane == HD, one, zero), query)
            QA[2 * t + 1, rr, :] = jnp.where(upper, query, jnp.where(lane == 0, one, zero))
            KA[2 * t, rr, :] = jnp.where(upper, jnp.where(lane == HD, fill, zero), keys)
            KA[2 * t + 1, rr, :] = jnp.where(upper, keys, jnp.where(lane == 0, fill, zero))
            VA[2 * t, rr, :] = jnp.where(upper, -one, vals)
            VA[2 * t + 1, rr, :] = jnp.where(upper, vals, -one)
            return carry

        lax.fori_loop(0, 4, shard, 0)

    rows_wait(X, s_x, r_x, 1)
    project(x_id, True)
    rows_wait(X, s_x, r_x, 2)
    rows_wait(X, s_x, r_x, 3)
    project(1 - x_id, False)

    def attend(p, carry):
        for c in range(2):
            rr = pl.ds(c * half, half)
            outs = []
            for e in range(2):
                h = 2 * p + e
                scores = nt(QA[h, rr, :], KA[h])
                top = jnp.max(scores, axis=1, keepdims=True)
                weight = jnp.exp(scores - top).astype(BF)
                PR[h, rr, :] = weight
                outs.append(nn(weight, VA[h]))
            inv = -1.0 / jnp.where(upper, pltpu.roll(outs[1], HD, 1), pltpu.roll(outs[0], HD, 1))
            LINV[p, rr, :] = inv
            MIX[p, rr, :] = (jnp.where(upper, outs[1], outs[0]) * inv).astype(BF)
        return carry

    lax.fori_loop(0, 4, attend, 0)

    for i in (3, 4, 5):
        w_wait(i, 2)
        w_forward(i).start()
    w_wait(3, 1)
    w_wait(3, 3)

    acc = nn(MIX[0], WO[0:LANES, :])
    for p in range(1, 4):
        acc = acc + nn(MIX[p], WO[p * LANES : (p + 1) * LANES, :])
    ACC[...] = acc

    step = total // 8
    gain0, gain1 = gain[0:1, :].astype(F32), gain[1:2, :].astype(F32)
    shift0, shift1 = shift[0:1, :].astype(F32), shift[1:2, :].astype(F32)
    ob0, ob1 = obias[0:1, :].astype(F32), obias[1:2, :].astype(F32)

    def norm_one(i, carry):
        rr = aligned(i, step)
        res = X[rr, :].astype(F32) + off + (ACC[rr, :] + ob0)
        cen = res - jnp.mean(res, axis=-1, keepdims=True)
        fac = lax.rsqrt(jnp.mean(cen * cen, axis=-1, keepdims=True) + EPSILON)
        nrm = cen * fac
        N1[rr, :] = nrm
        LIVE[rr, 1:2] = fac
        HL[rr, :] = (nrm * gain0 + shift0).astype(BF)
        return carry

    lax.fori_loop(0, 8, norm_one, 0)

    ACC[...] = jnp.zeros_like(ACC)

    def ffn(k, carry):
        t = flip(tp, k)

        @pl.when(k == 1)
        def _():
            w_wait(4, 1)
            w_wait(5, 1)

        @pl.when(k == 3)
        def _():
            w_wait(4, 3)
            w_wait(5, 3)

        for c in range(2):
            rr = pl.ds(c * half, half)
            upper_bias = jnp.concatenate([SB[t, 2 + i : 3 + i, :] for i in range(4)], axis=1)
            u = nn(HL[rr, :], WU[t]) + upper_bias
            sq = u * u
            th = jnp.tanh(u * (GELU_C + (GELU_C * 0.044715) * sq))
            hp = 0.5 + 0.5 * th
            act = (u * hp).astype(BF)
            ACT2[t, rr, :] = act
            GP[t, rr, :] = (
                hp + (0.5 * u) * (1.0 - th * th) * (GELU_C + (3.0 * GELU_C * 0.044715) * sq)
            ).astype(BF)
            ACC[rr, :] += nn(act, WD[t])
        return carry

    lax.fori_loop(0, 4, ffn, 0)

    for k in (1, 2, 3):
        rows_wait(COT, s_c, r_c, k)

    SM[...] = jnp.zeros_like(SM)

    def norm_two(i, carry):
        rr = aligned(i, step)
        hid = N1[rr, :] * gain0 + shift0
        res = hid + (ACC[rr, :] + ob1)
        cen = res - jnp.mean(res, axis=-1, keepdims=True)
        fac = lax.rsqrt(jnp.mean(cen * cen, axis=-1, keepdims=True) + EPSILON)
        nrm = cen * fac
        live = LIVE[rr, 0:1]
        gf = COT[rr, :].astype(F32) * live
        COT[rr, :] = ((nrm * gain1 + shift1) * live).astype(BF)
        gn = gf * gain1
        g2 = fac * (
            gn - jnp.mean(gn, axis=-1, keepdims=True) - nrm * jnp.mean(gn * nrm, axis=-1, keepdims=True)
        )
        ACC[rr, :] = g2
        G2L[rr, :] = g2.astype(BF)
        SM[5:6, :] += jnp.sum(gf * nrm, axis=0, keepdims=True)
        SM[7:8, :] += jnp.sum(gf, axis=0, keepdims=True)
        SM[9:10, :] += jnp.sum(g2, axis=0, keepdims=True)
        return carry

    lax.fori_loop(0, 8, norm_two, 0)

    def back_copy(buf, dst, ss, rs, k):
        return rcopy(buf.at[aligned(flip(tp, k), rows), :], dst.at[tp], ss.at[k], rs.at[k], tp_peer(k))

    def back_wait(buf, dst, ss, rs, k):
        there = dst.at[flip(tp, k)]
        rcopy(buf.at[aligned(tp, rows), :], there, ss.at[k], rs.at[k], tp_peer(k)).wait_recv()

    outs_sent = [back_copy(COT, out_rows, s_out, r_out, k) for k in (2, 3, 1)]
    for copy in outs_sent:
        copy.start()
    out_local = pltpu.make_async_copy(COT.at[aligned(tp, rows), :], out_rows.at[tp], s_loc.at[0])
    out_local.start()

    def gref(m, t):
        return WU.at[t] if m == 2 else G.at[m, t]

    def core_send(m, j):
        k = 1 if j == 0 else 3
        return rcopy(gref(m, flip(tp, k)), RC.at[m, j], s_rc.at[m, j], r_rc.at[m, j], tp_peer(1))

    def core_wait(m, j):
        rcopy(RC.at[m, j], RC.at[m, j], s_rc.at[m, j], r_rc.at[m, j], tp_peer(1)).wait_recv()

    def x_send(m):
        return rcopy(gref(m, flip(tp, 2)), RX.at[m], s_rx.at[m], r_rx.at[m], tp_peer(2))

    def reduce_early(m, k):
        @pl.when(k == 0)
        def _():
            core_send(m, 1).start()

        @pl.when(k == 1)
        def _():
            core_wait(m, 1)
            t = flip(tp, 2)
            ref = gref(m, t)
            ref[...] = (ref[...].astype(F32) + RC[m, 1].astype(F32)).astype(BF)
            x_send(m).start()

        @pl.when(k == 2)
        def _():
            core_send(m, 0).start()

    qrows = 512 // quad

    def quad_send(m, j):
        return rcopy(
            gref(m, tp).at[aligned(quad_at(j), qrows), :], RQ.at[m, j - 1], s_rq.at[m, j - 1], r_rq.at[m, j - 1],
            quad_peer(j),
        )

    def rest_send(m, j):
        return rcopy(RE.at[m, r_id], RE.at[m, r_id], s_re.at[m, j - 1], r_re.at[m, j - 1], rest_peer(j))

    def rest_wait(m, j):
        there = RE.at[m, lax.rem(r_id + rest_n - j, rest_n)]
        rcopy(there, there, s_re.at[m, j - 1], r_re.at[m, j - 1], rest_peer(j)).wait_recv()

    def ag_send(m, j):
        here = RX.at[m, aligned(q_id, qrows), :]
        return rcopy(here, here, s_ag.at[m, j - 1], r_ag.at[m, j - 1], quad_peer(j))

    def ag_wait(m, j):
        there = RX.at[m, aligned(quad_at(-j), qrows), :]
        rcopy(there, there, s_ag.at[m, j - 1], r_ag.at[m, j - 1], quad_peer(j)).wait_recv()

    def reduce_quad(m):
        core_wait(m, 0)
        rcopy(RX.at[m], RX.at[m], s_rx.at[m], r_rx.at[m], tp_peer(2)).wait_recv()
        ref = gref(m, tp)
        ref[...] = (ref[...].astype(F32) + RC[m, 0].astype(F32) + RX[m].astype(F32)).astype(BF)
        for j in range(1, quad):
            quad_send(m, j).start()

    def reduce_rest(m):
        for j in range(1, quad):
            quad_send(m, j).wait_recv()
        acc_q = gref(m, tp)[aligned(q_id, qrows), :].astype(F32)
        for j in range(quad - 1):
            acc_q = acc_q + RQ[m, j].astype(F32)
        RE[m, r_id] = acc_q.astype(BF)
        for j in range(1, rest_n):
            rest_send(m, j).start()

    def reduce_gather(m):
        for j in range(1, rest_n):
            rest_wait(m, j)
        acc_r = RE[m, 0].astype(F32)
        for j in range(1, rest_n):
            acc_r = acc_r + RE[m, j].astype(F32)
        RX[m, aligned(q_id, qrows), :] = acc_r.astype(BF)
        for j in range(1, quad):
            ag_send(m, j).start()

    def reduce_done(m):
        for j in range(1, quad):
            ag_wait(m, j)


    def ffn_back(k, carry):
        t = flip(tp, 3 - k)
        d_act = nt(G2L[...], WD[t])
        g_pre = d_act * GP[t].astype(F32)
        SM[pl.ds(10 + t, 1), :] = jnp.sum(g_pre, axis=0, keepdims=True)
        low = g_pre.astype(BF)
        GP[t] = low
        G[0, t] = tn(ACT2[t], G2L[...]).astype(BF)
        G[1, t] = tn(HL[...], low).astype(BF)
        ACC[...] += nt(low, WU[t])
        reduce_early(0, k)
        reduce_early(1, k)
        return carry

    lax.fori_loop(0, 4, ffn_back, 0)

    def norm_one_back(i, carry):
        rr = aligned(i, step)
        gh = ACC[rr, :]
        nrm = N1[rr, :]
        gn = gh * gain0
        g1 = LIVE[rr, 1:2] * (
            gn - jnp.mean(gn, axis=-1, keepdims=True) - nrm * jnp.mean(gn * nrm, axis=-1, keepdims=True)
        )
        ACC[rr, :] = g1
        G2L[rr, :] = g1.astype(BF)
        SM[4:5, :] += jnp.sum(gh * nrm, axis=0, keepdims=True)
        SM[6:7, :] += jnp.sum(gh, axis=0, keepdims=True)
        SM[8:9, :] += jnp.sum(g1, axis=0, keepdims=True)
        return carry

    lax.fori_loop(0, 8, norm_one_back, 0)

    def back_prep(p, carry):
        gm = nt(G2L[...], WO[aligned(p, LANES), :])
        WU[p, pl.ds(3 * LANES, LANES), :] = tn(MIX[p], G2L[...]).astype(BF)
        lane_f = lax.broadcasted_iota(jnp.int32, (total, LANES), 1)
        up_f = lane_f >= HD
        gs = gm * LINV[p]
        prod = gs * MIX[p].astype(F32)
        low = gs.astype(BF)
        for e in range(2):
            mine = up_f if e == 1 else jnp.logical_not(up_f)
            delta = jnp.sum(jnp.where(mine, prod, 0.0), axis=-1, keepdims=True)
            hi = delta.astype(BF)
            lo = (delta - hi.astype(F32)).astype(BF)
            base = HD * (1 - e)
            side = jnp.where(lane_f == base, hi, jnp.where(lane_f == base + 1, lo, zero))
            GP[p, :, pl.ds(e * LANES, LANES)] = jnp.where(mine, low, side)
        return carry

    w_forward(4).wait_send()
    lax.fori_loop(0, 4, back_prep, 0)

    ones = jnp.ones((8, total), BF)
    lane_f = lax.broadcasted_iota(jnp.int32, (total, LANES), 1)
    up_f = lane_f >= HD

    def attend_back(k, carry):
        p = flip(tp, 3 - k)
        d_k, d_v = [], []
        for c in range(2):
            rr = pl.ds(c * half, half)
            part = []
            for e in range(2):
                h = 2 * p + e
                go = GP[p, rr, pl.ds(e * LANES, LANES)]
                prob = PR[h, rr, :]
                d_s = (prob.astype(F32) * nt(go, VA[h])).astype(BF)
                part.append(nn(d_s, KA[h]))
                more = (tn(prob, go), tn(d_s, QA[h, rr, :]))
                if c == 0:
                    d_v.append(more[0])
                    d_k.append(more[1])
                else:
                    d_v[e] = d_v[e] + more[0]
                    d_k[e] = d_k[e] + more[1]
            ACT2[p, rr, 0:LANES] = (jnp.where(upper, part[1], part[0]) * 0.125).astype(BF)
        ACT2[p, :, LANES : 2 * LANES] = jnp.where(up_f, d_k[1], d_k[0]).astype(BF)
        ACT2[p, :, 2 * LANES : 3 * LANES] = jnp.where(up_f, d_v[1], d_v[0]).astype(BF)
        d_all = ACT2[p, :, 0 : 3 * LANES]
        WU[p, 0 : 3 * LANES, :] = tn(d_all, ACT[...]).astype(BF)
        sums = nn(ones, d_all)
        SM[14:15, aligned(p, LANES)] = sums[0:1, 0:LANES]
        SM[15:16, aligned(p, LANES)] = sums[0:1, 2 * LANES : 3 * LANES]
        reduce_early(2, k)

        @pl.when(k == 1)
        def _():
            reduce_quad(0)

        @pl.when(k == 2)
        def _():
            reduce_quad(1)

        @pl.when(k == 3)
        def _():
            reduce_rest(0)

        return carry

    lax.fori_loop(0, 4, attend_back, 0)

    reduce_quad(2)
    reduce_rest(1)
    reduce_gather(0)

    def input_grad(k, carry):
        b = flip(tp, 3 - k)
        rr = aligned(b, rows)
        grad = ACC[rr, :]
        for p in range(4):
            grad = grad + nt(ACT2[p, rr, 0 : 3 * LANES], WP[p])
        X[rr, :] = grad.astype(BF)
        SM[0:1, :] += jnp.sum(grad, axis=0, keepdims=True)

        @pl.when(k < 3)
        def _():
            kk = 3 - k
            rcopy(X.at[rr, :], ig_rows.at[tp], s_ig.at[kk], r_ig.at[kk], (dp, b)).start()

        return carry

    lax.fori_loop(0, 4, input_grad, 0)
    ig_local = pltpu.make_async_copy(X.at[aligned(tp, rows), :], ig_rows.at[tp], s_loc.at[1])
    ig_local.start()

    base_sum = SM[0:1, :]
    for c in range(dbias.shape[0]):
        SM[c : c + 1, :] = jnp.where(ds_here == c, 1.0, 0.0) * base_sum

    def sm_all(src, slots, me, count, sem0, peer_of, from_of):
        slots[me] = src
        copies = []
        for j in range(1, count):
            copies.append(rcopy(slots.at[me], slots.at[me], s_sm.at[sem0 + j], r_sm.at[sem0 + j], peer_of(j)))
        for copy in copies:
            copy.start()
        for j in range(1, count):
            there = slots.at[from_of(j)]
            rcopy(there, there, s_sm.at[sem0 + j], r_sm.at[sem0 + j], peer_of(j)).wait_recv()
        out = slots[0]
        for j in range(1, count):
            out = out + slots[j]
        return out, copies

    reduce_rest(2)
    reduce_gather(1)
    val, c1 = sm_all(SM[...], SMT, tp, 4, 0, tp_peer, lambda j: flip(tp, j))
    val, c2 = sm_all(val, SMQ, q_id, quad, 4, quad_peer, lambda j: quad_at(-j))
    reduce_gather(2)
    val, c3 = sm_all(val, SMR, r_id, rest_n, 4 + quad, rest_peer, lambda j: lax.rem(r_id + rest_n - j, rest_n))
    SM[...] = val
    g_dbias[...] = val[0:4, :]
    g_gain[...] = val[4:6, :]
    g_shift[...] = val[6:8, :]
    g_obias[...] = val[8:10, :]
    g_upb[...] = SM[pl.ds(10 + tp, 1), :]
    g_qvb[...] = SM[14:16, aligned(tp, LANES)]

    results = []

    def result(src, dst, i):
        results.append(pltpu.make_async_copy(src, dst, s_res.at[i]))
        results[-1].start()

    reduce_done(0)
    N1[0:width, :] = RX[0].astype(F32)
    result(N1.at[0:width, :], g_down, 0)
    reduce_done(1)
    ACC[0:width, :] = RX[1].astype(F32)
    result(ACC.at[0:width, :], g_up, 1)
    reduce_done(2)
    for i in range(3):
        LINV[i, 0:width, :] = jnp.transpose(RX[2, i * LANES : (i + 1) * LANES, :].astype(F32))
        result(LINV.at[i, 0:width, :], g_qkv.at[i], 2 + i)
    N1[width : width + LANES, :] = RX[2, 3 * LANES : 4 * LANES, :].astype(F32)
    result(N1.at[width : width + LANES, :], g_out, 5)
    for copy in results:
        copy.wait()

    for k in (1, 2, 3):
        back_wait(COT, out_rows, s_out, r_out, k)
        back_wait(X, ig_rows, s_ig, r_ig, k)
        back_copy(X, ig_rows, s_ig, r_ig, k).wait_send()
    ig_local.wait()
    out_local.wait()
    for copy in sends + outs_sent + c1 + c2 + c3:
        copy.wait_send()
    for i in (0, 1, 2, 3, 5):
        w_forward(i).wait_send()
    for m in range(3):
        core_send(m, 0).wait_send()
        core_send(m, 1).wait_send()
        x_send(m).wait_send()
        for j in range(1, quad):
            quad_send(m, j).wait_send()
            ag_send(m, j).wait_send()
        for j in range(1, rest_n):
            rest_send(m, j).wait_send()


def shards(dp_n, *args):
    (inputs, dataset, variate_mask, dataset_bias, w_qkv, qv_bias, w_out, out_bias, w_up, up_bias, w_down,
     norm_gain, norm_shift, cotangent) = args
    win, rows, width = inputs.shape
    total = variate_mask.shape[1]
    quad = 4 if dp_n <= 16 else 8
    rest_n = dp_n // quad
    ffs = w_up.shape[1]
    assert win == 4 and total == 4 * rows and width == 512 and ffs == 512 and w_out.shape[0] == LANES
    any_spec = pl.BlockSpec(memory_space=pl.ANY)
    vmem = pl.BlockSpec(memory_space=pltpu.VMEM)
    smem = pl.BlockSpec(memory_space=pltpu.SMEM)
    dma = pltpu.SemaphoreType.DMA
    V = pltpu.VMEM
    scratch = [
        V((total, width), BF),
        V((total, width), BF),
        V((4, width, 3 * LANES), BF),
        V((width, width), BF),
        V((4, width, ffs), BF),
        V((4, ffs, width), BF),
        V((4, 8, LANES), F32),
        V((total, width), BF),
        V((8, total, LANES), BF),
        V((8, total, LANES), BF),
        V((8, total, LANES), BF),
        V((8, total, total), BF),
        V((4, total, LANES), BF),
        V((4, total, LANES), F32),
        V((total, width), F32),
        V((total, width), BF),
        V((4, total, ffs), BF),
        V((4, total, ffs), BF),
        V((total, width), F32),
        V((total, width), BF),
        V((total, LANES), F32),
        V((2, 4, width, ffs), BF),
        V((3, 2, width, ffs), BF),
        V((3, width, ffs), BF),
        V((3, quad - 1, width // quad, ffs), BF),
        V((3, rest_n, width // quad, ffs), BF),
        V((16, width), F32),
        V((4, 16, width), F32),
        V((quad, 16, width), F32),
        V((rest_n, 16, width), F32),
        dma((8,)),
        dma((4,)), dma((4,)),
        dma((4,)), dma((4,)),
        dma((6, 4)), dma((6, 4)),
        dma((4,)), dma((4,)),
        dma((4,)), dma((4,)),
        dma((4,)), dma((4,)),
        dma((2,)),
        dma((3, 2)), dma((3, 2)),
        dma((3,)), dma((3,)),
        dma((3, quad - 1)), dma((3, quad - 1)),
        dma((3, max(rest_n - 1, 1))), dma((3, max(rest_n - 1, 1))),
        dma((3, quad - 1)), dma((3, quad - 1)),
        dma((4 + quad + rest_n,)), dma((4 + quad + rest_n,)),
        dma((6,)),
    ]
    sds = jax.ShapeDtypeStruct
    outs = pl.pallas_call(
        functools.partial(kernel, quad, rest_n),
        out_shape=(
            sds((win, rows, width), BF),
            sds((win, rows, width), BF),
            sds((3, width, LANES), F32),
            sds((LANES, width), F32),
            sds((width, ffs), F32),
            sds((ffs, width), F32),
            sds((4, width), F32),
            sds((2, width), F32),
            sds((2, width), F32),
            sds((2, width), F32),
            sds((1, width), F32),
            sds((2, LANES), F32),
        ),
        in_specs=[any_spec, any_spec, smem, vmem, vmem, any_spec, vmem, any_spec, vmem, any_spec, vmem, any_spec, vmem, vmem],
        out_specs=(any_spec,) * 6 + (vmem,) * 6,
        scratch_shapes=scratch,
        compiler_params=pltpu.CompilerParams(
            collective_id=0, has_side_effects=True, vmem_limit_bytes=65000000
        ),
        cost_estimate=pl.CostEstimate(flops=30 * 10**9, bytes_accessed=20 * 10**6, transcendentals=10**7),
        name="encoder_layer",
    )(inputs, cotangent, dataset, variate_mask, dataset_bias, w_qkv, qv_bias, w_out, out_bias, w_up,
      up_bias.reshape(4, LANES), w_down, norm_gain, norm_shift)
    (rows_out, rows_ig, g_qkv, g_out, g_up, g_down, g_dbias, g_gain, g_shift, g_obias, g_upb, g_qvb) = outs
    return (
        rows_out, rows_ig, g_dbias, g_qkv, g_qvb, g_out, g_obias, g_up, g_upb.reshape(-1), g_down, g_gain, g_shift,
    )


def solution(mesh):
    in_specs = (
        P("dp", "tp", None), P("dp"), P("dp", None), P(), P(None, None, "tp"), P(None, "tp"), P("tp", None), P(),
        P(None, "tp"), P("tp"), P("tp", None), P(), P(), P("dp", "tp", None),
    )
    out_specs = (
        P("dp", "tp", None), P("dp", "tp", None), P(), P(None, None, "tp"), P(None, "tp"), P("tp", None), P(),
        P(None, "tp"), P("tp"), P("tp", None), P(), P(),
    )
    body = functools.partial(shards, mesh.shape["dp"])
    return jax.shard_map(body, mesh=mesh, in_specs=in_specs, out_specs=out_specs, check_vma=False)
```

time: 621 us -> 157 us (0.25)
  waiting for transfers between devices: 361 us -> 0 us
  Pallas kernels: 0 us -> 143 us
  matrix products: 101 us -> 0 us
  blocking collectives: 63.4 us -> 0 us
  other arithmetic: 43.1 us -> 0 us
  local copies, waits for them, and re-layouts: 27.7 us -> 10.4 us
  between operations: 14.6 us -> 0.69 us
    reduce_scatter x4 -> x0, waiting for transfers between devices: 147 us -> none  [the longest x1 64.9 us: shards(): lax.psum_scatter(attn_part, 'tp', scatter_dimension=1, tiled=True)]
    pallas_call x0 -> x1, Pallas kernels: none -> 143 us  [shards(): pl.pallas_call(functools.partial(kernel, quad, rest_n), out_shape=(sds((w...]
    all_gather x4 -> x0, waiting for transfers between devices: 126 us -> none  [the longest x1 31.6 us: shards(): act_full = lax.all_gather(act_in, 'tp', axis=1, tiled=True)]
    dot_general x42 -> x0, matrix products: 101 us -> none  [the longest x8 9.59 us: masked_scores(): jnp.einsum('qhe,khe->hqk', q_heads, k_heads, preferred_element_type=jnp.f...]
    psum x1 -> x0, waiting for transfers between devices: 87.5 us -> none  [shards(): lax.psum((qkv_grad, qvb_grad, out_grad, up_grad, upb_grad, down_grad), 'dp')]
    psum x2 -> x0, blocking collectives: 63.4 us -> none  [the longest x1 41.4 us: shards(): lax.psum((bias_grad, jnp.stack([gain_one, gain_two]), jnp.stack([shift_on...]
    reduce_sum x12 -> x0, other arithmetic: 20.8 us -> none  [the longest x4 6.93 us: attend_window(): row_total = jnp.sum(exponent, axis=-1, keepdims=True)]
    convert_element_type x11 -> x0, other arithmetic: 18.3 us -> none  [the longest x4 8.98 us: attend_back(): score_low = grad_scores.astype(jnp.bfloat16)]
  transfers between devices with their start and end apart: 9 -> 0, of which waited for: 8 -> 0; matrix products, arithmetic and copies ran while one was open for 5% -> 0% of each run, Pallas kernels for 0% -> 0%
where the time goes in v1:
time: 157 us; the launch traced here: 154 us
  Pallas kernels  143 us (91%)
  local copies, waits for them, and re-layouts  10.4 us (7%)
    pallas_call x1, Pallas kernels, shards(): pl.pallas_call(functools.partial(kernel, quad, rest_n), out_shape=(sds((w...  143 us
    unnamed x34, local copies, waits for them, and re-layouts  10.4 us

profile of v1, /device:TPU:0, one launch (start us, length us, event | category | flops | bytes accessed | tf_op | source)
XLA Modules:
  0.0 154.2 jit_solution(15524178996776191478)
XLA Ops:
  0.6 143.2 %encoder_layer.1 = (bf16[4,224,512]{2,1,0:T(8,128)(2,1)}, bf16[4,224,512]{2,1,0:T(8,128)(2,1)}, f32[3,512,128]{2,1,0:T(8,128)}, f32[128,512]{1,0:T(8,128)}, f32[...) custom-call(bf16[4,224,512]{2,1,0:T(8,128)(2,1)} %x_in.1, ...), custom_call_target="tpu_custom_call" | custom-call | flops 30000001024 | bytes 20000000 | tf_op jit(solution)/shard_map/encoder_layer/pallas_call | solution.py:676
  143.8 0.0 copy-start.2
  143.8 2.2 %copy.38 = bf16[4,224,512]{2,1,0:T(8,128)(2,1)} copy(bf16[4,224,512]{2,1,0:T(8,128)(2,1)} %get-tuple-element.48) | data formatting | bytes 1835008
  146.1 0.0 copy-done.2
  146.1 0.9 copy.39
  147.0 0.0 copy-done.5
  147.0 0.6 copy.40
  147.6 0.0 copy-done.3
  147.6 0.9 copy.41
  148.5 0.0 copy-done.10
  148.5 0.6 copy.42
  149.1 0.0 copy-done.4
  149.1 0.7 copy.43
  149.8 0.0 copy-done.8
  149.8 0.6 copy.44
  150.4 1.0 copy.45
  151.3 0.0 copy-done.9
  151.3 0.6 copy.46
  151.9 0.1 copy-done
  152.0 1.0 copy.47
  152.9 0.0 copy-done.7
  152.9 0.6 copy.48
  153.5 0.1 copy-done.6
  153.6 0.6 copy.49
  (11 shorter events, 0.0 us)
Async XLA Ops:
  143.8 2.3 %copy-start.2 = (bf16[4,224,512]{2,1,0:T(8,128)(2,1)S(1)}, bf16[4,224,512]{2,1,0:T(8,128)(2,1)}, u32[]{:S(2)}) copy-start(bf16[4,224,512]{2,1,0:T(8,128)(2,1)} %get-tuple-element.49) | copy-start | bytes 2752516
  146.1 0.9 copy-start.5
  146.1 1.5 copy-start.3
  147.6 0.9 copy-start.10
  147.6 1.5 copy-start.4
  147.6 2.8 %copy-start.1 = (f32[512,512]{1,0:T(8,128)S(1)}, f32[512,512]{1,0:T(8,128)}, u32[]{:S(2)}) copy-start(f32[512,512]{1,0:T(8,128)} %get-tuple-element.55) | copy-start | bytes 3145732
  149.1 0.7 copy-start.8
  150.4 1.0 copy-start.9
  150.4 1.6 %copy-start = (f32[512,512]{1,0:T(8,128)S(1)}, f32[512,512]{1,0:T(8,128)}, u32[]{:S(2)}) copy-start(f32[512,512]{1,0:T(8,128)} %get-tuple-element.57) | copy-start | bytes 3145732
  152.0 1.0 copy-start.7
  152.9 0.7 copy-start.6

commit v2 on v1

--- a/solution.py
+++ b/solution.py
@@ -43,10 +43,10 @@
 def kernel(
     quad, rest_n,
     x_in, cot_in, dataset, mask, dbias, w_qkv, qvb, w_out, obias, w_up, upb, w_down, gain, shift,
-    out_rows, ig_rows, g_qkv, g_out, g_up, g_down, g_dbias, g_gain, g_shift, g_obias, g_upb, g_qvb,
+    out_rows, ig_rows, g_sum, g_small,
     X, COT, WP, WO, WU, WD, SB, ACT, QA, KA, VA, PR, MIX, LINV, N1, HL, ACT2, GP, ACC, G2L, LIVE,
     G, RC, RX, RQ, RE, SM, SMT, SMQ, SMR,
-    s_own, s_x, r_x, s_c, r_c, s_w, r_w, s_b, r_b, s_out, r_out, s_ig, r_ig, s_loc,
+    s_own, s_x, r_x, s_c, r_c, s_wx, r_wx, s_wq, r_wq, s_wf, r_wf, s_wc, r_wc, s_b, r_b, s_out, r_out, s_ig, r_ig, s_loc,
     s_rc, r_rc, s_rx, r_rx, s_rq, r_rq, s_re, r_re, s_ag, r_ag, s_sm, r_sm, s_res,
 ):
     dp = lax.axis_index("dp")
@@ -95,24 +95,69 @@
     SB[tp, 2:6, :] = upb[...].astype(F32)
     pl.semaphore_wait(barrier, len(peers))
 
-    def weight_slices(t):
-        return [WP.at[t, :, pl.ds(i * LANES, LANES)] for i in range(3)] + [
-            WO.at[aligned(t, LANES), :], WU.at[t], WD.at[t]
-        ]
-
-    w_src = [w_qkv.at[0], w_qkv.at[1], w_qkv.at[2], w_out, w_up, w_down]
-    w_dst = weight_slices(tp)
-
-    def w_send(i, k):
-        return rcopy(w_src[i], w_dst[i], s_w.at[i, k], r_w.at[i, k], tp_peer(k))
-
-    def w_wait(i, k):
-        dst = weight_slices(flip(tp, k))[i]
-        rcopy(dst, dst, s_w.at[i, k], r_w.at[i, k], tp_peer(k)).wait_recv()
-
-    def w_forward(i):
-        dst = weight_slices(flip(tp, 2))[i]
-        return rcopy(dst, dst, s_w.at[i, 3], r_w.at[i, 3], tp_peer(1))
+    wq = width // quad
+    oq = LANES // quad
+
+    def w_whole(g, t):
+        return (WP.at[t], WO.at[aligned(t, LANES), :], WU.at[t], WD.at[t])[g]
+
+    def w_part(g, t, q):
+        if g == 1:
+            return WO.at[pl.ds(pl.multiple_of(t * LANES + q * oq, oq), oq), :]
+        return (WP, WO, WU, WD)[g].at[t, aligned(q, wq), :]
+
+    def wx_dst(i, t):
+        if i < 3:
+            return WP.at[t, aligned(q_id, wq), pl.ds(i * LANES, LANES)]
+        return w_part(i - 2, t, q_id)
+
+    wx_src = [w_qkv.at[i, aligned(q_id, wq), :] for i in range(3)]
+    wx_src += [w_out.at[aligned(q_id, oq), :], w_up.at[aligned(q_id, wq), :], w_down.at[aligned(q_id, wq), :]]
+    members = {0: (0, 1, 2), 1: (3,), 2: (4,), 3: (5,)}
+
+    def wx_send(i):
+        return rcopy(wx_src[i], wx_dst(i, tp), s_wx.at[i], r_wx.at[i], tp_peer(2))
+
+    def wx_wait(g):
+        for i in members[g]:
+            there = wx_dst(i, flip(tp, 2))
+            rcopy(there, there, s_wx.at[i], r_wx.at[i], tp_peer(2)).wait_recv()
+
+    def wq_send(g, j):
+        here = w_part(g, flip(tp, 2), q_id)
+        return rcopy(here, here, s_wq.at[g, j - 1], r_wq.at[g, j - 1], quad_peer(j))
+
+    def wq_start(g):
+        wx_wait(g)
+        for j in range(1, quad):
+            wq_send(g, j).start()
+
+    def wf_send(g):
+        here = w_whole(g, flip(tp, 2))
+        return rcopy(here, here, s_wf.at[g], r_wf.at[g], tp_peer(1))
+
+    def wf_start(g):
+        for j in range(1, quad):
+            there = w_part(g, flip(tp, 2), quad_at(-j))
+            rcopy(there, there, s_wq.at[g, j - 1], r_wq.at[g, j - 1], quad_peer(j)).wait_recv()
+        wf_send(g).start()
+
+    def wf_wait(g):
+        there = w_whole(g, flip(tp, 3))
+        rcopy(there, there, s_wf.at[g], r_wf.at[g], tp_peer(1)).wait_recv()
+
+    def wc_dst(i, t):
+        return WP.at[t, :, pl.ds(i * LANES, LANES)] if i < 3 else w_whole(i - 2, t)
+
+    wc_src = [w_qkv.at[0], w_qkv.at[1], w_qkv.at[2], w_out, w_up, w_down]
+
+    def wc_send(i):
+        return rcopy(wc_src[i], wc_dst(i, tp), s_wc.at[i], r_wc.at[i], tp_peer(1))
+
+    def wc_wait(g):
+        for i in members[g]:
+            there = wc_dst(i, flip(tp, 1))
+            rcopy(there, there, s_wc.at[i], r_wc.at[i], tp_peer(1)).wait_recv()
 
     def rows_copy(src, dst, ss, rs, k):
         return rcopy(src.at[flip(tp, k)], dst.at[aligned(tp, rows), :], ss.at[k], rs.at[k], tp_peer(k))
@@ -127,14 +172,15 @@
     sends = []
     for k in (1, 2, 3):
         sends.append(sb_copy(k))
-    for i in range(3):
-        sends.append(w_send(i, 2))
-        sends.append(w_send(i, 1))
+    for i in range(4):
+        sends.append(wx_send(i))
+    for i in range(4):
+        sends.append(wc_send(i))
     for k in (2, 3, 1):
         sends.append(rows_copy(x_in, X, s_x, r_x, k))
-    for i in (3, 4, 5):
-        sends.append(w_send(i, 2))
-        sends.append(w_send(i, 1))
+    for i in (4, 5):
+        sends.append(wx_send(i))
+        sends.append(wc_send(i))
     for k in (2, 3, 1):
         sends.append(rows_copy(cot_in, COT, s_c, r_c, k))
     for copy in sends:
@@ -169,19 +215,16 @@
             if first:
                 @pl.when(k == 1)
                 def _():
-                    for i in range(3):
-                        w_wait(i, 1)
+                    wc_wait(0)
 
                 @pl.when(k == 2)
                 def _():
-                    for i in range(3):
-                        w_wait(i, 2)
-                        w_forward(i).start()
+                    wf_start(0)
+                    wf_start(1)
 
                 @pl.when(k == 3)
                 def _():
-                    for i in range(3):
-                        w_wait(i, 3)
+                    wf_wait(0)
 
             qkv = nn(ACT[rr, :], WP[t])
             query = (qkv[:, :LANES] + SB[t, 0:1, :]).astype(BF) * BF(0.125)
@@ -197,6 +240,8 @@
 
         lax.fori_loop(0, 4, shard, 0)
 
+    wq_start(0)
+    wq_start(1)
     rows_wait(X, s_x, r_x, 1)
     project(x_id, True)
     rows_wait(X, s_x, r_x, 2)
@@ -204,6 +249,11 @@
     project(1 - x_id, False)
 
     def attend(p, carry):
+        @pl.when(p == 2)
+        def _():
+            wq_start(2)
+            wq_start(3)
+
         for c in range(2):
             rr = pl.ds(c * half, half)
             outs = []
@@ -221,11 +271,8 @@
 
     lax.fori_loop(0, 4, attend, 0)
 
-    for i in (3, 4, 5):
-        w_wait(i, 2)
-        w_forward(i).start()
-    w_wait(3, 1)
-    w_wait(3, 3)
+    wc_wait(1)
+    wf_wait(1)
 
     acc = nn(MIX[0], WO[0:LANES, :])
     for p in range(1, 4):
@@ -257,13 +304,18 @@
 
         @pl.when(k == 1)
         def _():
-            w_wait(4, 1)
-            w_wait(5, 1)
+            wc_wait(2)
+            wc_wait(3)
+
+        @pl.when(k == 2)
+        def _():
+            wf_start(2)
+            wf_start(3)
 
         @pl.when(k == 3)
         def _():
-            w_wait(4, 3)
-            w_wait(5, 3)
+            wf_wait(2)
+            wf_wait(3)
 
         for c in range(2):
             rr = pl.ds(c * half, half)
@@ -460,7 +512,9 @@
             GP[p, :, pl.ds(e * LANES, LANES)] = jnp.where(mine, low, side)
         return carry
 
-    w_forward(4).wait_send()
+    wf_send(2).wait_send()
+    for j in range(1, quad):
+        wq_send(2, j).wait_send()
     lax.fori_loop(0, 4, back_prep, 0)
 
     ones = jnp.ones((8, total), BF)
@@ -561,34 +615,12 @@
     val, c2 = sm_all(val, SMQ, q_id, quad, 4, quad_peer, lambda j: quad_at(-j))
     reduce_gather(2)
     val, c3 = sm_all(val, SMR, r_id, rest_n, 4 + quad, rest_peer, lambda j: lax.rem(r_id + rest_n - j, rest_n))
-    SM[...] = val
-    g_dbias[...] = val[0:4, :]
-    g_gain[...] = val[4:6, :]
-    g_shift[...] = val[6:8, :]
-    g_obias[...] = val[8:10, :]
-    g_upb[...] = SM[pl.ds(10 + tp, 1), :]
-    g_qvb[...] = SM[14:16, aligned(tp, LANES)]
-
-    results = []
-
-    def result(src, dst, i):
-        results.append(pltpu.make_async_copy(src, dst, s_res.at[i]))
-        results[-1].start()
-
-    reduce_done(0)
-    N1[0:width, :] = RX[0].astype(F32)
-    result(N1.at[0:width, :], g_down, 0)
-    reduce_done(1)
-    ACC[0:width, :] = RX[1].astype(F32)
-    result(ACC.at[0:width, :], g_up, 1)
-    reduce_done(2)
-    for i in range(3):
-        LINV[i, 0:width, :] = jnp.transpose(RX[2, i * LANES : (i + 1) * LANES, :].astype(F32))
-        result(LINV.at[i, 0:width, :], g_qkv.at[i], 2 + i)
-    N1[width : width + LANES, :] = RX[2, 3 * LANES : 4 * LANES, :].astype(F32)
-    result(N1.at[width : width + LANES, :], g_out, 5)
-    for copy in results:
-        copy.wait()
+    g_small[...] = val
+
+    for m in range(3):
+        reduce_done(m)
+    result = pltpu.make_async_copy(RX, g_sum, s_res)
+    result.start()
 
     for k in (1, 2, 3):
         back_wait(COT, out_rows, s_out, r_out, k)
@@ -596,10 +628,13 @@
         back_copy(X, ig_rows, s_ig, r_ig, k).wait_send()
     ig_local.wait()
     out_local.wait()
+    result.wait()
     for copy in sends + outs_sent + c1 + c2 + c3:
         copy.wait_send()
-    for i in (0, 1, 2, 3, 5):
-        w_forward(i).wait_send()
+    for g in (0, 1, 3):
+        wf_send(g).wait_send()
+        for j in range(1, quad):
+            wq_send(g, j).wait_send()
     for m in range(3):
         core_send(m, 0).wait_send()
         core_send(m, 1).wait_send()
@@ -609,6 +644,35 @@
             ag_send(m, j).wait_send()
         for j in range(1, rest_n):
             rest_send(m, j).wait_send()
+
+
+def finish(
+    raw_out, raw_ig, g_sum, g_small,
+    out_rows, ig_rows, g_qkv, g_out, g_up, g_down, g_dbias, g_gain, g_shift, g_obias, g_upb, g_qvb,
+):
+    i = pl.program_id(0)
+    tp = lax.axis_index("tp")
+    out_rows[...] = raw_out[...]
+    ig_rows[...] = raw_ig[...]
+    g_down[...] = g_sum[0].astype(F32)
+    g_up[...] = g_sum[1].astype(F32)
+
+    @pl.when(i < 3)
+    def _():
+        g_qkv[0] = jnp.transpose(g_sum[2].astype(F32))
+
+    @pl.when(i == 3)
+    def _():
+        g_out[...] = g_sum[2].astype(F32)
+
+    @pl.when(i == 0)
+    def _():
+        g_dbias[...] = g_small[0:4, :]
+        g_gain[...] = g_small[4:6, :]
+        g_shift[...] = g_small[6:8, :]
+        g_obias[...] = g_small[8:10, :]
+        g_upb[...] = g_small[pl.ds(10 + tp, 1), :]
+        g_qvb[...] = g_small[14:16, aligned(tp, LANES)]
 
 
 def shards(dp_n, *args):
@@ -659,7 +723,10 @@
         dma((8,)),
         dma((4,)), dma((4,)),
         dma((4,)), dma((4,)),
-        dma((6, 4)), dma((6, 4)),
+        dma((6,)), dma((6,)),
+        dma((4, quad - 1)), dma((4, quad - 1)),
+        dma((4,)), dma((4,)),
+        dma((6,)), dma((6,)),
         dma((4,)), dma((4,)),
         dma((4,)), dma((4,)),
         dma((4,)), dma((4,)),
@@ -670,11 +737,30 @@
         dma((3, max(rest_n - 1, 1))), dma((3, max(rest_n - 1, 1))),
         dma((3, quad - 1)), dma((3, quad - 1)),
         dma((4 + quad + rest_n,)), dma((4 + quad + rest_n,)),
-        dma((6,)),
+        dma,
     ]
     sds = jax.ShapeDtypeStruct
     outs = pl.pallas_call(
         functools.partial(kernel, quad, rest_n),
+        out_shape=(
+            sds((win, rows, width), BF),
+            sds((win, rows, width), BF),
+            sds((3, width, ffs), BF),
+            sds((16, width), F32),
+        ),
+        in_specs=[any_spec, any_spec, smem, vmem, vmem, any_spec, vmem, any_spec, vmem, any_spec, vmem, any_spec, vmem, vmem],
+        out_specs=(any_spec,) * 3 + (vmem,),
+        scratch_shapes=scratch,
+        compiler_params=pltpu.CompilerParams(
+            collective_id=0, has_side_effects=True, vmem_limit_bytes=65000000
+        ),
+        cost_estimate=pl.CostEstimate(flops=30 * 10**9, bytes_accessed=20 * 10**6, transcendentals=10**7),
+        name="encoder_layer",
+    )(inputs, cotangent, dataset, variate_mask, dataset_bias, w_qkv, qv_bias, w_out, out_bias, w_up,
+      up_bias.reshape(4, LANES), w_down, norm_gain, norm_shift)
+    raw_out, raw_ig, g_sum, g_small = outs
+    res = pl.pallas_call(
+        finish,
         out_shape=(
             sds((win, rows, width), BF),
             sds((win, rows, width), BF),
@@ -689,17 +775,30 @@
             sds((1, width), F32),
             sds((2, LANES), F32),
         ),
-        in_specs=[any_spec, any_spec, smem, vmem, vmem, any_spec, vmem, any_spec, vmem, any_spec, vmem, any_spec, vmem, vmem],
-        out_specs=(any_spec,) * 6 + (vmem,) * 6,
-        scratch_shapes=scratch,
-        compiler_params=pltpu.CompilerParams(
-            collective_id=0, has_side_effects=True, vmem_limit_bytes=65000000
+        grid=(4,),
+        in_specs=[
+            pl.BlockSpec((1, rows, width), lambda i: (i, 0, 0)),
+            pl.BlockSpec((1, rows, width), lambda i: (i, 0, 0)),
+            pl.BlockSpec((3, LANES, ffs), lambda i: (0, i, 0)),
+            pl.BlockSpec((16, width), lambda i: (0, 0)),
+        ],
+        out_specs=(
+            pl.BlockSpec((1, rows, width), lambda i: (i, 0, 0)),
+            pl.BlockSpec((1, rows, width), lambda i: (i, 0, 0)),
+            pl.BlockSpec((1, width, LANES), lambda i: (jnp.minimum(i, 2), 0, 0)),
+            pl.BlockSpec((LANES, width), lambda i: (0, 0)),
+            pl.BlockSpec((LANES, ffs), lambda i: (i, 0)),
+            pl.BlockSpec((LANES, width), lambda i: (i, 0)),
+            pl.BlockSpec((4, width), lambda i: (0, 0)),
+            pl.BlockSpec((2, width), lambda i: (0, 0)),
+            pl.BlockSpec((2, width), lambda i: (0, 0)),
+            pl.BlockSpec((2, width), lambda i: (0, 0)),
+            pl.BlockSpec((1, width), lambda i: (0, 0)),
+            pl.BlockSpec((2, LANES), lambda i: (0, 0)),
         ),
-        cost_estimate=pl.CostEstimate(flops=30 * 10**9, bytes_accessed=20 * 10**6, transcendentals=10**7),
-        name="encoder_layer",
-    )(inputs, cotangent, dataset, variate_mask, dataset_bias, w_qkv, qv_bias, w_out, out_bias, w_up,
-      up_bias.reshape(4, LANES), w_down, norm_gain, norm_shift)
-    (rows_out, rows_ig, g_qkv, g_out, g_up, g_down, g_dbias, g_gain, g_shift, g_obias, g_upb, g_qvb) = outs
+        name="write_results",
+    )(raw_out, raw_ig, g_sum, g_small)
+    (rows_out, rows_ig, g_qkv, g_out, g_up, g_down, g_dbias, g_gain, g_shift, g_obias, g_upb, g_qvb) = res
     return (
         rows_out, rows_ig, g_dbias, g_qkv, g_qvb, g_out, g_obias, g_up, g_upb.reshape(-1), g_down, g_gain, g_shift,
     )

time: 157 us -> 136 us (0.87)
  local copies, waits for them, and re-layouts: 10.4 us -> 0 us
  Pallas kernels: 143 us -> 134 us
    pallas_call x1, Pallas kernels: 143 us -> 129 us  [shards(): pl.pallas_call(functools.partial(kernel, quad, rest_n), out_shape=(sds((w...]
    unnamed x34 -> x0, local copies, waits for them, and re-layouts: 10.4 us -> none
    pallas_call x0 -> x1, Pallas kernels: none -> 5.1 us  [shards(): pl.pallas_call(finish, out_shape=(sds((win, rows, width), BF), sds((win,...]
where the time goes in v2:
time: 136 us; the launch traced here: 135 us
  Pallas kernels  134 us (99%)
    pallas_call x1, Pallas kernels, shards(): pl.pallas_call(functools.partial(kernel, quad, rest_n), out_shape=(sds((w...  129 us
    pallas_call x1, Pallas kernels, shards(): pl.pallas_call(finish, out_shape=(sds((win, rows, width), BF), sds((win,...  5.1 us

profile of v2, /device:TPU:0, one launch (start us, length us, event | category | flops | bytes accessed | tf_op | source)
XLA Modules:
  0.0 134.7 jit_solution(2356386997902313782)
XLA Ops:
  0.6 128.7 %encoder_layer.1 = (bf16[4,224,512]{2,1,0:T(8,128)(2,1)}, bf16[4,224,512]{2,1,0:T(8,128)(2,1)}, bf16[3,512,512]{2,1,0:T(8,128)(2,1)}, f32[16,512]{1,0:T(8,128)}) custom-call(bf16[4,224,512]{2,1,0:T(8,128)(2,1)} %x_in.1, bf16[4,224,512]{2,1,0:T(8,128)(2,1)} %cot_in.1, s32[4]{0:T(128)} %dataset.1, s32[4,896]{1,0:T(4,128)} %mask.1, bf16[4,512]{1,0:T(4,128)(2,1)} %dbias.1, ...), custom_call_target="tpu_custom_call" | custom-call | flops 30000001024 | bytes 20000000 | tf_op jit(solution)/shard_map/encoder_layer/pallas_call | solution.py:743
  129.4 5.1 %write_results.1 = (bf16[4,224,512]{2,1,0:T(8,128)(2,1)}, bf16[4,224,512]{2,1,0:T(8,128)(2,1)}, f32[3,512,128]{2,1,0:T(8,128)}, f32[128,512]{1,0:T(8,128)}, f32[...) custom-call(bf16[4,224,512]{2,1,0:T(8,128)(2,1)} %get-tuple-element., ...), custom_call_target="tpu_custom_call" | custom-call | tf_op jit(solution)/shard_map/write_results/pallas_call | solution.py:762

commit v3 on v2

--- a/solution.py
+++ b/solution.py
@@ -45,9 +45,9 @@
     x_in, cot_in, dataset, mask, dbias, w_qkv, qvb, w_out, obias, w_up, upb, w_down, gain, shift,
     out_rows, ig_rows, g_sum, g_small,
     X, COT, WP, WO, WU, WD, SB, ACT, QA, KA, VA, PR, MIX, LINV, N1, HL, ACT2, GP, ACC, G2L, LIVE,
-    G, RC, RX, RQ, RE, SM, SMT, SMQ, SMR,
+    G, RC, RX, RQ, RB, RE, SD, SM, SMT, SMQ, SMR,
     s_own, s_x, r_x, s_c, r_c, s_wx, r_wx, s_wq, r_wq, s_wf, r_wf, s_wc, r_wc, s_b, r_b, s_out, r_out, s_ig, r_ig, s_loc,
-    s_rc, r_rc, s_rx, r_rx, s_rq, r_rq, s_re, r_re, s_ag, r_ag, s_sm, r_sm, s_res,
+    s_rc, r_rc, s_rx, r_rx, s_rq, r_rq, s_rb, r_rb, s_re, r_re, s_ag, r_ag, s_sm, r_sm, s_res,
 ):
     dp = lax.axis_index("dp")
     tp = lax.axis_index("tp")
@@ -370,95 +370,119 @@
         rcopy(buf.at[aligned(tp, rows), :], there, ss.at[k], rs.at[k], tp_peer(k)).wait_recv()
 
     outs_sent = [back_copy(COT, out_rows, s_out, r_out, k) for k in (2, 3, 1)]
-    for copy in outs_sent:
-        copy.start()
+    outs_sent[0].start()
+    outs_sent[2].start()
     out_local = pltpu.make_async_copy(COT.at[aligned(tp, rows), :], out_rows.at[tp], s_loc.at[0])
     out_local.start()
 
-    def gref(m, t):
-        return WU.at[t] if m == 2 else G.at[m, t]
-
-    def core_send(m, j):
-        k = 1 if j == 0 else 3
-        return rcopy(gref(m, flip(tp, k)), RC.at[m, j], s_rc.at[m, j], r_rc.at[m, j], tp_peer(1))
-
-    def core_wait(m, j):
-        rcopy(RC.at[m, j], RC.at[m, j], s_rc.at[m, j], r_rc.at[m, j], tp_peer(1)).wait_recv()
-
-    def x_send(m):
-        return rcopy(gref(m, flip(tp, 2)), RX.at[m], s_rx.at[m], r_rx.at[m], tp_peer(2))
-
-    def reduce_early(m, k):
-        @pl.when(k == 0)
-        def _():
-            core_send(m, 1).start()
-
-        @pl.when(k == 1)
-        def _():
-            core_wait(m, 1)
-            t = flip(tp, 2)
-            ref = gref(m, t)
-            ref[...] = (ref[...].astype(F32) + RC[m, 1].astype(F32)).astype(BF)
-            x_send(m).start()
-
-        @pl.when(k == 2)
-        def _():
-            core_send(m, 0).start()
-
-    qrows = 512 // quad
-
-    def quad_send(m, j):
-        return rcopy(
-            gref(m, tp).at[aligned(quad_at(j), qrows), :], RQ.at[m, j - 1], s_rq.at[m, j - 1], r_rq.at[m, j - 1],
-            quad_peer(j),
-        )
-
-    def rest_send(m, j):
-        return rcopy(RE.at[m, r_id], RE.at[m, r_id], s_re.at[m, j - 1], r_re.at[m, j - 1], rest_peer(j))
-
-    def rest_wait(m, j):
-        there = RE.at[m, lax.rem(r_id + rest_n - j, rest_n)]
-        rcopy(there, there, s_re.at[m, j - 1], r_re.at[m, j - 1], rest_peer(j)).wait_recv()
-
-    def ag_send(m, j):
-        here = RX.at[m, aligned(q_id, qrows), :]
-        return rcopy(here, here, s_ag.at[m, j - 1], r_ag.at[m, j - 1], quad_peer(j))
-
-    def ag_wait(m, j):
-        there = RX.at[m, aligned(quad_at(-j), qrows), :]
-        rcopy(there, there, s_ag.at[m, j - 1], r_ag.at[m, j - 1], quad_peer(j)).wait_recv()
-
-    def reduce_quad(m):
-        core_wait(m, 0)
-        rcopy(RX.at[m], RX.at[m], s_rx.at[m], r_rx.at[m], tp_peer(2)).wait_recv()
-        ref = gref(m, tp)
-        ref[...] = (ref[...].astype(F32) + RC[m, 0].astype(F32) + RX[m].astype(F32)).astype(BF)
+    pieces = ((0, 0, width), (1, 0, width)) + tuple((2, g * LANES, LANES) for g in (3, 2, 1, 0))
+
+    def gref(i, t):
+        m, r0, n = pieces[i]
+        return WU.at[t, pl.ds(r0, n), :] if m == 2 else G.at[m, t]
+
+    def gchunk(i, t, q):
+        m, r0, n = pieces[i]
+        at = pl.ds(pl.multiple_of(r0 + q * (n // quad), 16), n // quad)
+        return WU.at[t, at, :] if m == 2 else G.at[m, t, at, :]
+
+    def rxchunk(i, q):
+        m, r0, n = pieces[i]
+        return RX.at[m, pl.ds(pl.multiple_of(r0 + q * (n // quad), 16), n // quad), :]
+
+    def span(i):
+        return pl.ds(pieces[i][1], pieces[i][2])
+
+    def qspan(i):
+        return pl.ds(pieces[i][1] // quad, pieces[i][2] // quad)
+
+    def core_send(i, j):
+        there = RC.at[pieces[i][0], j, span(i), :]
+        return rcopy(gref(i, flip(tp, 1 if j == 0 else 3)), there, s_rc.at[i, j], r_rc.at[i, j], tp_peer(1))
+
+    def core_add(i, j):
+        there = RC.at[pieces[i][0], j, span(i), :]
+        rcopy(there, there, s_rc.at[i, j], r_rc.at[i, j], tp_peer(1)).wait_recv()
+        ref = gref(i, flip(tp, 2) if j == 1 else tp)
+        ref[...] = (ref[...].astype(F32) + there[...].astype(F32)).astype(BF)
+
+    def x_send(i):
+        if i == 1:
+            src, dst = gchunk(i, flip(tp, 2), q_id), rxchunk(i, q_id)
+        else:
+            src, dst = gref(i, flip(tp, 2)), RX.at[pieces[i][0], span(i), :]
+        return rcopy(src, dst, s_rx.at[i], r_rx.at[i], tp_peer(2))
+
+    def quad_send(i, j, other=False):
+        if other:
+            return rcopy(gchunk(i, flip(tp, 2), quad_at(j)), RB.at[j - 1], s_rb.at[j - 1], r_rb.at[j - 1], quad_peer(j))
+        there = RQ.at[pieces[i][0], j - 1, qspan(i), :]
+        return rcopy(gchunk(i, tp, quad_at(j)), there, s_rq.at[i, j - 1], r_rq.at[i, j - 1], quad_peer(j))
+
+    def quad_start(i, other=False):
         for j in range(1, quad):
-            quad_send(m, j).start()
-
-    def reduce_rest(m):
+            quad_send(i, j, other).start()
+
+    def rest_send(i, j):
+        here = RE.at[pieces[i][0], r_id, qspan(i), :]
+        return rcopy(here, here, s_re.at[i, j - 1], r_re.at[i, j - 1], rest_peer(j))
+
+    def ag_send(i, j):
+        here = rxchunk(i, q_id)
+        return rcopy(here, here, s_ag.at[i, j - 1], r_ag.at[i, j - 1], quad_peer(j))
+
+    def reduce_x(i):
+        core_add(i, 1)
+        x_send(i).start()
+
+    def reduce_quad(i):
+        core_add(i, 0)
+        x_send(i).wait_recv()
+        ref = gref(i, tp)
+        ref[...] = (ref[...].astype(F32) + RX[pieces[i][0], span(i), :].astype(F32)).astype(BF)
+        quad_start(i)
+
+    def reduce_other(i):
         for j in range(1, quad):
-            quad_send(m, j).wait_recv()
-        acc_q = gref(m, tp)[aligned(q_id, qrows), :].astype(F32)
+            quad_send(i, j, True).wait_recv()
+        ref = gchunk(i, flip(tp, 2), q_id)
+        acc_q = ref[...].astype(F32)
         for j in range(quad - 1):
-            acc_q = acc_q + RQ[m, j].astype(F32)
-        RE[m, r_id] = acc_q.astype(BF)
+            acc_q = acc_q + RB[j].astype(F32)
+        ref[...] = acc_q.astype(BF)
+        x_send(i).start()
+
+    def reduce_rest(i):
+        m = pieces[i][0]
+        for j in range(1, quad):
+            quad_send(i, j).wait_recv()
+        acc_q = gchunk(i, tp, q_id)[...].astype(F32)
+        for j in range(quad - 1):
+            acc_q = acc_q + RQ[m, j, qspan(i), :].astype(F32)
+        if i == 1:
+            x_send(i).wait_recv()
+            acc_q = acc_q + rxchunk(i, q_id)[...].astype(F32)
+        RE[m, r_id, qspan(i), :] = acc_q.astype(BF)
         for j in range(1, rest_n):
-            rest_send(m, j).start()
-
-    def reduce_gather(m):
+            rest_send(i, j).start()
+
+    def reduce_gather(i):
+        m = pieces[i][0]
         for j in range(1, rest_n):
-            rest_wait(m, j)
-        acc_r = RE[m, 0].astype(F32)
+            there = RE.at[m, lax.rem(r_id + rest_n - j, rest_n), qspan(i), :]
+            rcopy(there, there, s_re.at[i, j - 1], r_re.at[i, j - 1], rest_peer(j)).wait_recv()
+        acc_r = RE[m, 0, qspan(i), :].astype(F32)
         for j in range(1, rest_n):
-            acc_r = acc_r + RE[m, j].astype(F32)
-        RX[m, aligned(q_id, qrows), :] = acc_r.astype(BF)
+            acc_r = acc_r + RE[m, j, qspan(i), :].astype(F32)
+        here = rxchunk(i, q_id)
+        here[...] = acc_r.astype(BF)
         for j in range(1, quad):
-            ag_send(m, j).start()
-
-    def reduce_done(m):
+            ag_send(i, j).start()
+
+    def reduce_done(i):
         for j in range(1, quad):
-            ag_wait(m, j)
+            there = rxchunk(i, quad_at(-j))
+            rcopy(there, there, s_ag.at[i, j - 1], r_ag.at[i, j - 1], quad_peer(j)).wait_recv()
 
 
     def ffn_back(k, carry):
@@ -471,8 +495,28 @@
         G[0, t] = tn(ACT2[t], G2L[...]).astype(BF)
         G[1, t] = tn(HL[...], low).astype(BF)
         ACC[...] += nt(low, WU[t])
-        reduce_early(0, k)
-        reduce_early(1, k)
+
+        @pl.when(k == 0)
+        def _():
+            core_send(0, 1).start()
+            core_send(1, 1).start()
+
+        @pl.when(k == 1)
+        def _():
+            reduce_x(0)
+            core_add(1, 1)
+            quad_start(1, True)
+
+        @pl.when(k == 2)
+        def _():
+            core_send(0, 0).start()
+            core_send(1, 0).start()
+
+        @pl.when(k == 3)
+        def _():
+            core_add(1, 0)
+            quad_start(1)
+
         return carry
 
     lax.fori_loop(0, 4, ffn_back, 0)
@@ -516,6 +560,9 @@
     for j in range(1, quad):
         wq_send(2, j).wait_send()
     lax.fori_loop(0, 4, back_prep, 0)
+    core_send(2, 1).start()
+    core_send(2, 0).start()
+    reduce_other(1)
 
     ones = jnp.ones((8, total), BF)
     lane_f = lax.broadcasted_iota(jnp.int32, (total, LANES), 1)
@@ -523,52 +570,125 @@
 
     def attend_back(k, carry):
         p = flip(tp, 3 - k)
-        d_k, d_v = [], []
-        for c in range(2):
-            rr = pl.ds(c * half, half)
-            part = []
-            for e in range(2):
-                h = 2 * p + e
-                go = GP[p, rr, pl.ds(e * LANES, LANES)]
-                prob = PR[h, rr, :]
-                d_s = (prob.astype(F32) * nt(go, VA[h])).astype(BF)
-                part.append(nn(d_s, KA[h]))
-                more = (tn(prob, go), tn(d_s, QA[h, rr, :]))
-                if c == 0:
-                    d_v.append(more[0])
-                    d_k.append(more[1])
-                else:
-                    d_v[e] = d_v[e] + more[0]
-                    d_k[e] = d_k[e] + more[1]
-            ACT2[p, rr, 0:LANES] = (jnp.where(upper, part[1], part[0]) * 0.125).astype(BF)
-        ACT2[p, :, LANES : 2 * LANES] = jnp.where(up_f, d_k[1], d_k[0]).astype(BF)
-        ACT2[p, :, 2 * LANES : 3 * LANES] = jnp.where(up_f, d_v[1], d_v[0]).astype(BF)
-        d_all = ACT2[p, :, 0 : 3 * LANES]
-        WU[p, 0 : 3 * LANES, :] = tn(d_all, ACT[...]).astype(BF)
-        sums = nn(ones, d_all)
-        SM[14:15, aligned(p, LANES)] = sums[0:1, 0:LANES]
-        SM[15:16, aligned(p, LANES)] = sums[0:1, 2 * LANES : 3 * LANES]
-        reduce_early(2, k)
-
-        @pl.when(k == 1)
-        def _():
-            reduce_quad(0)
-
-        @pl.when(k == 2)
-        def _():
-            reduce_quad(1)
-
-        @pl.when(k == 3)
-        def _():
-            reduce_rest(0)
-
+
+        def at(where, what):
+            @pl.when(k == where)
+            def _():
+                for fun in what:
+                    fun()
+
+        def join(cols, group):
+            low = jnp.where(up_f, cols[1], cols[0]).astype(BF)
+            ACT2[p, :, group * LANES : (group + 1) * LANES] = low
+            WU[p, group * LANES : (group + 1) * LANES, :] = tn(low, ACT[...]).astype(BF)
+            SD[p, 0:1, group * LANES : (group + 1) * LANES] = jnp.sum(low.astype(F32), axis=0, keepdims=True)
+
+        def join_t(parts, group):
+            low_t = jnp.concatenate([parts[0][:HD], parts[1][HD:]], axis=0).astype(BF)
+            WU[p, group * LANES : (group + 1) * LANES, :] = nn(low_t, ACT[...]).astype(BF)
+            low = jnp.transpose(low_t)
+            ACT2[p, :, group * LANES : (group + 1) * LANES] = low
+            SD[p, 0:1, group * LANES : (group + 1) * LANES] = jnp.sum(low.astype(F32), axis=0, keepdims=True)
+
+        def hooks(step):
+            for where, todo in enumerate(plan[step]):
+                if todo:
+                    at(where, todo)
+
+        cols = []
+        for e in range(2):
+            cols.append(tn(GP[p, :, pl.ds(e * LANES, LANES)], PR[2 * p + e]))
+        join_t(cols, 2)
+        hooks(0)
+        cols = []
+        for e in range(2):
+            h = 2 * p + e
+            for c in range(2):
+                rr = pl.ds(c * half, half)
+                d_p = nt(GP[p, rr, pl.ds(e * LANES, LANES)], VA[h])
+                PR[h, rr, :] = (PR[h, rr, :].astype(F32) * d_p).astype(BF)
+            cols.append(tn(QA[h], PR[h]))
+        join_t(cols, 1)
+        hooks(1)
+        cols = []
+        for e in range(2):
+            h = 2 * p + e
+            cols.append(nn(PR[h], KA[h]) * 0.125)
+        join(cols, 0)
+        hooks(2)
         return carry
 
+    def act(fun, *args):
+        return lambda: fun(*args)
+
+    def send(fun, *args):
+        return lambda: fun(*args).start()
+
+    plan = (
+        (
+            (send(core_send, 3, 1), act(reduce_x, 2)),
+            (act(reduce_x, 3),),
+            (send(core_send, 3, 0), act(reduce_quad, 2)),
+            (act(reduce_quad, 3), act(reduce_rest, 2)),
+        ),
+        (
+            (send(core_send, 4, 1),),
+            (act(reduce_x, 4),),
+            (send(core_send, 4, 0),),
+            (act(reduce_quad, 4),),
+        ),
+        (
+            (send(core_send, 5, 1), act(reduce_quad, 0)),
+            (act(reduce_x, 5), outs_sent[1].start, act(reduce_rest, 1)),
+            (send(core_send, 5, 0), act(reduce_rest, 0)),
+            (act(reduce_quad, 5),),
+        ),
+    )
     lax.fori_loop(0, 4, attend_back, 0)
 
-    reduce_quad(2)
-    reduce_rest(1)
-    reduce_gather(0)
+    base_sum = SM[8:9, :]
+    for p in range(4):
+        sums = jnp.broadcast_to(SD[p, 0:1, :], (8, 3 * LANES))
+        SM[14:15, p * LANES : (p + 1) * LANES] = sums[0:1, 0:LANES]
+        SM[15:16, p * LANES : (p + 1) * LANES] = sums[0:1, 2 * LANES : 3 * LANES]
+        hi = sums.astype(BF)
+        rem = sums - hi.astype(F32)
+        mid = rem.astype(BF)
+        low = (rem - mid.astype(F32)).astype(BF)
+        for term in (hi, mid, low):
+            base_sum = base_sum + nt(term, WP[p])[0:1, :]
+    for c in range(dbias.shape[0]):
+        SM[c : c + 1, :] = jnp.where(ds_here == c, 1.0, 0.0) * base_sum
+
+    stages = (
+        (SMT, tp, 4, 0, tp_peer, lambda j: flip(tp, j)),
+        (SMQ, q_id, quad, 4, quad_peer, lambda j: quad_at(-j)),
+        (SMR, r_id, rest_n, 4 + quad, rest_peer, lambda j: lax.rem(r_id + rest_n - j, rest_n)),
+    )
+
+    def sm_send(stage, j):
+        slots, me, count, sem0, peer_of, from_of = stages[stage]
+        return rcopy(slots.at[me], slots.at[me], s_sm.at[sem0 + j], r_sm.at[sem0 + j], peer_of(j))
+
+    def sm_start(stage, value):
+        slots, me, count, sem0, peer_of, from_of = stages[stage]
+        slots[me] = value
+        for j in range(1, count):
+            sm_send(stage, j).start()
+
+    def sm_sum(stage):
+        slots, me, count, sem0, peer_of, from_of = stages[stage]
+        for j in range(1, count):
+            there = slots.at[from_of(j)]
+            rcopy(there, there, s_sm.at[sem0 + j], r_sm.at[sem0 + j], peer_of(j)).wait_recv()
+        value = slots[0]
+        for j in range(1, count):
+            value = value + slots[j]
+        return value
+
+    sm_start(0, SM[...])
+    reduce_gather(1)
+    reduce_gather(2)
 
     def input_grad(k, carry):
         b = flip(tp, 3 - k)
@@ -577,7 +697,6 @@
         for p in range(4):
             grad = grad + nt(ACT2[p, rr, 0 : 3 * LANES], WP[p])
         X[rr, :] = grad.astype(BF)
-        SM[0:1, :] += jnp.sum(grad, axis=0, keepdims=True)
 
         @pl.when(k < 3)
         def _():
@@ -590,35 +709,18 @@
     ig_local = pltpu.make_async_copy(X.at[aligned(tp, rows), :], ig_rows.at[tp], s_loc.at[1])
     ig_local.start()
 
-    base_sum = SM[0:1, :]
-    for c in range(dbias.shape[0]):
-        SM[c : c + 1, :] = jnp.where(ds_here == c, 1.0, 0.0) * base_sum
-
-    def sm_all(src, slots, me, count, sem0, peer_of, from_of):
-        slots[me] = src
-        copies = []
-        for j in range(1, count):
-            copies.append(rcopy(slots.at[me], slots.at[me], s_sm.at[sem0 + j], r_sm.at[sem0 + j], peer_of(j)))
-        for copy in copies:
-            copy.start()
-        for j in range(1, count):
-            there = slots.at[from_of(j)]
-            rcopy(there, there, s_sm.at[sem0 + j], r_sm.at[sem0 + j], peer_of(j)).wait_recv()
-        out = slots[0]
-        for j in range(1, count):
-            out = out + slots[j]
-        return out, copies
-
-    reduce_rest(2)
-    reduce_gather(1)
-    val, c1 = sm_all(SM[...], SMT, tp, 4, 0, tp_peer, lambda j: flip(tp, j))
-    val, c2 = sm_all(val, SMQ, q_id, quad, 4, quad_peer, lambda j: quad_at(-j))
-    reduce_gather(2)
-    val, c3 = sm_all(val, SMR, r_id, rest_n, 4 + quad, rest_peer, lambda j: lax.rem(r_id + rest_n - j, rest_n))
-    g_small[...] = val
-
-    for m in range(3):
-        reduce_done(m)
+    sm_start(1, sm_sum(0))
+    reduce_rest(3)
+    reduce_rest(4)
+    reduce_rest(5)
+    reduce_gather(0)
+    sm_start(2, sm_sum(1))
+    reduce_gather(3)
+    reduce_gather(4)
+    reduce_gather(5)
+    g_small[...] = sm_sum(2)
+    for i in range(6):
+        reduce_done(i)
     result = pltpu.make_async_copy(RX, g_sum, s_res)
     result.start()
 
@@ -629,21 +731,26 @@
     ig_local.wait()
     out_local.wait()
     result.wait()
-    for copy in sends + outs_sent + c1 + c2 + c3:
+    for copy in sends + outs_sent:
         copy.wait_send()
+    for stage in range(3):
+        for j in range(1, stages[stage][2]):
+            sm_send(stage, j).wait_send()
     for g in (0, 1, 3):
         wf_send(g).wait_send()
         for j in range(1, quad):
             wq_send(g, j).wait_send()
-    for m in range(3):
-        core_send(m, 0).wait_send()
-        core_send(m, 1).wait_send()
-        x_send(m).wait_send()
+    for i in range(6):
+        core_send(i, 0).wait_send()
+        core_send(i, 1).wait_send()
+        x_send(i).wait_send()
         for j in range(1, quad):
-            quad_send(m, j).wait_send()
-            ag_send(m, j).wait_send()
+            quad_send(i, j).wait_send()
+            ag_send(i, j).wait_send()
+            if i == 1:
+                quad_send(i, j, True).wait_send()
         for j in range(1, rest_n):
-            rest_send(m, j).wait_send()
+            rest_send(i, j).wait_send()
 
 
 def finish(
@@ -715,7 +822,9 @@
         V((3, 2, width, ffs), BF),
         V((3, width, ffs), BF),
         V((3, quad - 1, width // quad, ffs), BF),
+        V((quad - 1, width // quad, ffs), BF),
         V((3, rest_n, width // quad, ffs), BF),
+        V((4, 8, 3 * LANES), F32),
         V((16, width), F32),
         V((4, 16, width), F32),
         V((quad, 16, width), F32),
@@ -731,11 +840,12 @@
         dma((4,)), dma((4,)),
         dma((4,)), dma((4,)),
         dma((2,)),
-        dma((3, 2)), dma((3, 2)),
-        dma((3,)), dma((3,)),
-        dma((3, quad - 1)), dma((3, quad - 1)),
-        dma((3, max(rest_n - 1, 1))), dma((3, max(rest_n - 1, 1))),
-        dma((3, quad - 1)), dma((3, quad - 1)),
+        dma((6, 2)), dma((6, 2)),
+        dma((6,)), dma((6,)),
+        dma((6, quad - 1)), dma((6, quad - 1)),
+        dma((quad - 1,)), dma((quad - 1,)),
+        dma((6, max(rest_n - 1, 1))), dma((6, max(rest_n - 1, 1))),
+        dma((6, quad - 1)), dma((6, quad - 1)),
         dma((4 + quad + rest_n,)), dma((4 + quad + rest_n,)),
         dma,
     ]

time: 136 us -> 119 us (0.88)
  Pallas kernels: 134 us -> 118 us
    pallas_call x1, Pallas kernels: 129 us -> 113 us  [shards(): pl.pallas_call(functools.partial(kernel, quad, rest_n), out_shape=(sds((w...]
where the time goes in v3:
time: 119 us
  Pallas kernels  118 us (99%)
    pallas_call x1, Pallas kernels, shards(): pl.pallas_call(functools.partial(kernel, quad, rest_n), out_shape=(sds((w...  113 us
    pallas_call x1, Pallas kernels, shards(): pl.pallas_call(finish, out_shape=(sds((win, rows, width), BF), sds((win,...  5.1 us

profile of v3, /device:TPU:0, one launch (start us, length us, event | category | flops | bytes accessed | tf_op | source)
XLA Modules:
  0.0 119.0 jit_solution(14697130371491490154)
XLA Ops:
  0.6 113.1 %encoder_layer.1 = (bf16[4,224,512]{2,1,0:T(8,128)(2,1)}, bf16[4,224,512]{2,1,0:T(8,128)(2,1)}, bf16[3,512,512]{2,1,0:T(8,128)(2,1)}, f32[16,512]{1,0:T(8,128)}) custom-call(bf16[4,224,512]{2,1,0:T(8,128)(2,1)} %x_in.1, bf16[4,224,512]{2,1,0:T(8,128)(2,1)} %cot_in.1, s32[4]{0:T(128)} %dataset.1, s32[4,896]{1,0:T(4,128)} %mask.1, bf16[4,512]{1,0:T(4,128)(2,1)} %dbias.1, ...), custom_call_target="tpu_custom_call" | custom-call | flops 30000001024 | bytes 20000000 | tf_op jit(solution)/shard_map/encoder_layer/pallas_call | solution.py:853
  113.7 5.1 %write_results.1 = (bf16[4,224,512]{2,1,0:T(8,128)(2,1)}, bf16[4,224,512]{2,1,0:T(8,128)(2,1)}, f32[3,512,128]{2,1,0:T(8,128)}, f32[128,512]{1,0:T(8,128)}, f32[...) custom-call(bf16[4,224,512]{2,1,0:T(8,128)(2,1)} %get-tuple-element., ...), custom_call_target="tpu_custom_call" | custom-call | tf_op jit(solution)/shard_map/write_results/pallas_call | solution.py:872

commit v4 on v3

--- a/solution.py
+++ b/solution.py
@@ -279,7 +279,7 @@
         acc = acc + nn(MIX[p], WO[p * LANES : (p + 1) * LANES, :])
     ACC[...] = acc
 
-    step = total // 8
+    step = total // 2
     gain0, gain1 = gain[0:1, :].astype(F32), gain[1:2, :].astype(F32)
     shift0, shift1 = shift[0:1, :].astype(F32), shift[1:2, :].astype(F32)
     ob0, ob1 = obias[0:1, :].astype(F32), obias[1:2, :].astype(F32)
@@ -295,7 +295,7 @@
         HL[rr, :] = (nrm * gain0 + shift0).astype(BF)
         return carry
 
-    lax.fori_loop(0, 8, norm_one, 0)
+    lax.fori_loop(0, 2, norm_one, 0)
 
     ACC[...] = jnp.zeros_like(ACC)
 
@@ -360,7 +360,7 @@
         SM[9:10, :] += jnp.sum(g2, axis=0, keepdims=True)
         return carry
 
-    lax.fori_loop(0, 8, norm_two, 0)
+    lax.fori_loop(0, 2, norm_two, 0)
 
     def back_copy(buf, dst, ss, rs, k):
         return rcopy(buf.at[aligned(flip(tp, k), rows), :], dst.at[tp], ss.at[k], rs.at[k], tp_peer(k))
@@ -536,7 +536,7 @@
         SM[8:9, :] += jnp.sum(g1, axis=0, keepdims=True)
         return carry
 
-    lax.fori_loop(0, 8, norm_one_back, 0)
+    lax.fori_loop(0, 2, norm_one_back, 0)
 
     def back_prep(p, carry):
         gm = nt(G2L[...], WO[aligned(p, LANES), :])
@@ -718,19 +718,22 @@
     reduce_gather(3)
     reduce_gather(4)
     reduce_gather(5)
+    results = []
+    for m, done in enumerate(((0,), (1,), (2, 3, 4, 5))):
+        for i in done:
+            reduce_done(i)
+        results.append(pltpu.make_async_copy(RX.at[m], g_sum.at[m], s_res.at[m]))
+        results[-1].start()
+
     g_small[...] = sm_sum(2)
-    for i in range(6):
-        reduce_done(i)
-    result = pltpu.make_async_copy(RX, g_sum, s_res)
-    result.start()
-
     for k in (1, 2, 3):
         back_wait(COT, out_rows, s_out, r_out, k)
         back_wait(X, ig_rows, s_ig, r_ig, k)
         back_copy(X, ig_rows, s_ig, r_ig, k).wait_send()
     ig_local.wait()
     out_local.wait()
-    result.wait()
+    for result in results:
+        result.wait()
     for copy in sends + outs_sent:
         copy.wait_send()
     for stage in range(3):
@@ -847,7 +850,7 @@
         dma((6, max(rest_n - 1, 1))), dma((6, max(rest_n - 1, 1))),
         dma((6, quad - 1)), dma((6, quad - 1)),
         dma((4 + quad + rest_n,)), dma((4 + quad + rest_n,)),
-        dma,
+        dma((3,)),
     ]
     sds = jax.ShapeDtypeStruct
     outs = pl.pallas_call(

time: 119 us -> 117 us (0.983)
  Pallas kernels: 118 us -> 116 us
    pallas_call x1, Pallas kernels: 113 us -> 111 us  [shards(): pl.pallas_call(functools.partial(kernel, quad, rest_n), out_shape=(sds((w...]
where the time goes in v4:
time: 117 us; the launch traced here: 116 us
  Pallas kernels  116 us (99%)
    pallas_call x1, Pallas kernels, shards(): pl.pallas_call(functools.partial(kernel, quad, rest_n), out_shape=(sds((w...  111 us
    pallas_call x1, Pallas kernels, shards(): pl.pallas_call(finish, out_shape=(sds((win, rows, width), BF), sds((win,...  5.1 us

profile of v4, /device:TPU:0, one launch (start us, length us, event | category | flops | bytes accessed | tf_op | source)
XLA Modules:
  0.0 116.5 jit_solution(9900933388685123338)
XLA Ops:
  0.6 110.5 %encoder_layer.1 = (bf16[4,224,512]{2,1,0:T(8,128)(2,1)}, bf16[4,224,512]{2,1,0:T(8,128)(2,1)}, bf16[3,512,512]{2,1,0:T(8,128)(2,1)}, f32[16,512]{1,0:T(8,128)}) custom-call(bf16[4,224,512]{2,1,0:T(8,128)(2,1)} %x_in.1, bf16[4,224,512]{2,1,0:T(8,128)(2,1)} %cot_in.1, s32[4]{0:T(128)} %dataset.1, s32[4,896]{1,0:T(4,128)} %mask.1, bf16[4,512]{1,0:T(4,128)(2,1)} %dbias.1, ...), custom_call_target="tpu_custom_call" | custom-call | flops 30000001024 | bytes 20000000 | tf_op jit(solution)/shard_map/encoder_layer/pallas_call | solution.py:856
  111.2 5.1 %write_results.1 = (bf16[4,224,512]{2,1,0:T(8,128)(2,1)}, bf16[4,224,512]{2,1,0:T(8,128)(2,1)}, f32[3,512,128]{2,1,0:T(8,128)}, f32[128,512]{1,0:T(8,128)}, f32[...) custom-call(bf16[4,224,512]{2,1,0:T(8,128)(2,1)} %get-tuple-element., ...), custom_call_target="tpu_custom_call" | custom-call | tf_op jit(solution)/shard_map/write_results/pallas_call | solution.py:875

commit v5 on v4

--- a/solution.py
+++ b/solution.py
@@ -292,12 +292,13 @@
         nrm = cen * fac
         N1[rr, :] = nrm
         LIVE[rr, 1:2] = fac
-        HL[rr, :] = (nrm * gain0 + shift0).astype(BF)
+        hid = nrm * gain0 + shift0
+        HL[rr, :] = hid.astype(BF)
+        ACC[rr, :] = hid + ob1
         return carry
 
     lax.fori_loop(0, 2, norm_one, 0)
 
-    ACC[...] = jnp.zeros_like(ACC)
 
     def ffn(k, carry):
         t = flip(tp, k)
@@ -341,8 +342,7 @@
 
     def norm_two(i, carry):
         rr = aligned(i, step)
-        hid = N1[rr, :] * gain0 + shift0
-        res = hid + (ACC[rr, :] + ob1)
+        res = ACC[rr, :]
         cen = res - jnp.mean(res, axis=-1, keepdims=True)
         fac = lax.rsqrt(jnp.mean(cen * cen, axis=-1, keepdims=True) + EPSILON)
         nrm = cen * fac

time: 117 us -> 117 us (level)
  no operation moved by 1% of the time
where the time goes in v5:
time: 117 us; the launch traced here: 116 us
  Pallas kernels  115 us (98%)
    pallas_call x1, Pallas kernels, shards(): pl.pallas_call(functools.partial(kernel, quad, rest_n), out_shape=(sds((w...  110 us
    pallas_call x1, Pallas kernels, shards(): pl.pallas_call(finish, out_shape=(sds((win, rows, width), BF), sds((win,...  5.1 us

profile of v5, /device:TPU:0, one launch (start us, length us, event | category | flops | bytes accessed | tf_op | source)
XLA Modules:
  0.0 116.3 jit_solution(4114268186684444502)
XLA Ops:
  0.6 110.3 %encoder_layer.1 = (bf16[4,224,512]{2,1,0:T(8,128)(2,1)}, bf16[4,224,512]{2,1,0:T(8,128)(2,1)}, bf16[3,512,512]{2,1,0:T(8,128)(2,1)}, f32[16,512]{1,0:T(8,128)}) custom-call(bf16[4,224,512]{2,1,0:T(8,128)(2,1)} %x_in.1, bf16[4,224,512]{2,1,0:T(8,128)(2,1)} %cot_in.1, s32[4]{0:T(128)} %dataset.1, s32[4,896]{1,0:T(4,128)} %mask.1, bf16[4,512]{1,0:T(4,128)(2,1)} %dbias.1, ...), custom_call_target="tpu_custom_call" | custom-call | flops 30000001024 | bytes 20000000 | tf_op jit(solution)/shard_map/encoder_layer/pallas_call | solution.py:856
  111.0 5.1 %write_results.1 = (bf16[4,224,512]{2,1,0:T(8,128)(2,1)}, bf16[4,224,512]{2,1,0:T(8,128)(2,1)}, f32[3,512,128]{2,1,0:T(8,128)}, f32[128,512]{1,0:T(8,128)}, f32[...) custom-call(bf16[4,224,512]{2,1,0:T(8,128)(2,1)} %get-tuple-element., ...), custom_call_target="tpu_custom_call" | custom-call | tf_op jit(solution)/shard_map/write_results/pallas_call | solution.py:875
